TPU v7x, 32 devices: a whole 2x2x4 slice. The times are simulated.
32 devices in a mesh: dp: 8 (over z, y), mp: 4 (over x, core).
Axes of the slice: x: 2, y: 2, z: 4, core: 2. Of those that a mesh axis runs over, the one named last changes fastest.
Arguments:
- dec_in: bfloat16 [2, 512, 768], P(None, 'dp'), may hold values from -6 to 6
- encoded: bfloat16 [2, 98304, 768], P(None, 'dp'), may hold values from -6 to 6
- seg_lengths: int32 [2, 8, 64], P(None, 'dp'), may hold values from 1 to 512, 12288 in all within a row
- pair_slot: int32 [2, 512], replicated, may hold values from 0 to 511, as said below
- relevance: float32 [2, 512], P(None, 'dp'), may hold values from -6 to 6
- score_dir: bfloat16 [768], replicated, may hold values from -0.21875 to 0.21875
- gain_self: bfloat16 [768], P('dp'), may hold values from 0.5 to 1.5
- gain_cross: bfloat16 [768], P('dp'), may hold values from 0.5 to 1.5
- gain_ff: bfloat16 [768], P('dp'), may hold values from 0.5 to 1.5
- self_value: bfloat16 [768, 768], P('dp', 'mp'), may hold values from -0.21875 to 0.21875
- self_out: bfloat16 [768, 768], P('mp', 'dp'), may hold values from -0.21875 to 0.21875
- cross_query: bfloat16 [768, 768], P('dp', 'mp'), may hold values from -0.0546875 to 0.0546875
- cross_key: bfloat16 [768, 768], P('dp', 'mp'), may hold values from -0.21875 to 0.21875
- cross_value: bfloat16 [768, 768], P('dp', 'mp'), may hold values from -0.21875 to 0.21875
- cross_out: bfloat16 [768, 768], P('mp', 'dp'), may hold values from -1.25 to 1.25
- ff_in: bfloat16 [768, 3072], P('dp', 'mp'), may hold values from -0.21875 to 0.21875
- ff_out: bfloat16 [3072, 768], P('mp', 'dp'), may hold values from -0.109375 to 0.109375
Outputs:
- dec_out: float32 [2, 512, 768], P(None, 'dp')
- d_dec_in: float32 [2, 512, 768], P(None, 'dp')
- d_encoded: bfloat16 [2, 98304, 768], P(None, ('dp', 'mp'))
- g_gain_self: float32 [768], P('dp')
- g_gain_cross: float32 [768], P('dp')
- g_gain_ff: float32 [768], P('dp')
- g_self_value: float32 [768, 768], P('dp', 'mp')
- g_self_out: float32 [768, 768], P('mp', 'dp')
- g_cross_query: float32 [768, 768], P('dp', 'mp')
- g_cross_key: float32 [768, 768], P('dp', 'mp')
- g_cross_value: float32 [768, 768], P('dp', 'mp')
- g_cross_out: float32 [768, 768], P('mp', 'dp')
- g_ff_in: float32 [768, 3072], P('dp', 'mp')
- g_ff_out: float32 [3072, 768], P('mp', 'dp')
Inputs may be any that keep to these rules, and one draw needn't show every extreme that they name: `seg_lengths`: each row holds the segment lengths of the 64 pairs of one index of dp in one micro-batch; a row sums to 12288 and its largest entry is 512. `pair_slot`: for each micro-batch a permutation of the 512 pairs onto slots; slot r belongs to query r // 16 and to index r // 64 of dp; of the 64 pairs of each index of dp exactly 8 go to slots of each index.
All inputs are finite; a program needn't handle non-finite values.
Results may differ from a plain program's by a relative error of at most 0.04.
Values may be sent and summed in bfloat16 or wider, within the bound.
A program may use at most 256 MiB of HBM per device.

v0:
```python
import math

import jax
import jax.numpy as jnp
from jax import lax
from jax.sharding import PartitionSpec as P

D = 768
HEAD_DIM = 64
CAND = 16


norm_eps = 1e-06


def lower(values):
    return values.astype(jnp.bfloat16)


def product(left, right, form):
    return jnp.einsum(form, left, right, preferred_element_type=jnp.float32)


def norm_forward(values, gain_row):
    inv_scale = lax.rsqrt(jnp.mean(values * values, axis=-1, keepdims=True) + norm_eps)
    return (values * inv_scale * gain_row, inv_scale)


def norm_backward(values, inv_scale, gain_row, upstream):
    unit_rows = values * inv_scale
    grad_gain = jnp.sum(upstream * unit_rows, axis=0)
    pushed = upstream * gain_row
    return (
        inv_scale * (pushed - unit_rows * jnp.mean(pushed * unit_rows, axis=-1, keepdims=True)),
        grad_gain,
    )


def head_total(partial_value):
    return lax.psum(partial_value, "mp")


def spread_rows(inside, table):
    return jnp.sum(jnp.where(inside, table[None, :, :], 0.0), axis=1)


def fetch(
    gain_self,
    gain_cross,
    gain_ff,
    self_value,
    self_out,
    cross_query,
    cross_key,
    cross_value,
    cross_out,
    ff_in,
    ff_out,
):
    gathered = (
        lax.all_gather(gain_self, "dp", axis=0, tiled=True),
        lax.all_gather(gain_cross, "dp", axis=0, tiled=True),
        lax.all_gather(gain_ff, "dp", axis=0, tiled=True),
        lax.all_gather(self_value, "dp", axis=0, tiled=True),
        lax.all_gather(cross_query, "dp", axis=0, tiled=True),
        lax.all_gather(cross_key, "dp", axis=0, tiled=True),
        lax.all_gather(cross_value, "dp", axis=0, tiled=True),
        lax.all_gather(ff_in, "dp", axis=0, tiled=True),
        lax.all_gather(self_out, "dp", axis=1, tiled=True),
        lax.all_gather(cross_out, "dp", axis=1, tiled=True),
        lax.all_gather(ff_out, "dp", axis=1, tiled=True),
    )
    key_full, value_full = (
        lax.all_gather(gathered[5], "mp", axis=1, tiled=True),
        lax.all_gather(gathered[6], "mp", axis=1, tiled=True),
    )
    return tuple(gathered) + (key_full, value_full)


def shards(
    dec_in,
    encoded,
    seg_lengths,
    pair_slot,
    relevance,
    score_dir,
    gain_self,
    gain_cross,
    gain_ff,
    self_value,
    self_out,
    cross_query,
    cross_key,
    cross_value,
    cross_out,
    ff_in,
    ff_out,
):
    micro_count = dec_in.shape[0]
    pair_count = dec_in.shape[1]
    tokens = encoded.shape[1]
    groups = lax.axis_size("dp")
    member_rank = lax.axis_index("dp")
    per_peer = pair_count // groups
    direction = score_dir.astype(jnp.float32)
    loss_weight = CAND * math.sqrt(D)
    positions = jnp.arange(tokens, dtype=jnp.int32)[:, None]
    local_index = jnp.arange(pair_count, dtype=jnp.int32)
    stored = None
    outputs = []
    grads_in = []
    grads_enc = []
    totals = None
    for micro_index in range(micro_count):
        stored = fetch(
            gain_self,
            gain_cross,
            gain_ff,
            self_value,
            self_out,
            cross_query,
            cross_key,
            cross_value,
            cross_out,
            ff_in,
            ff_out,
        )
        (
            gain_one,
            gain_two,
            gain_three,
            w_self_value,
            w_query,
            w_key,
            w_value,
            w_ff_in,
            w_self_out,
            w_cross_out,
            w_ff_out,
            key_full,
            value_full,
        ) = stored
        gain_one = gain_one.astype(jnp.float32)
        gain_two = gain_two.astype(jnp.float32)
        gain_three = gain_three.astype(jnp.float32)
        stream_in = dec_in[micro_index].astype(jnp.float32)
        encoder_rows = encoded[micro_index]
        lengths = seg_lengths[micro_index, 0]
        seg_ends = jnp.cumsum(lengths)
        starts = seg_ends - lengths
        member = (positions >= starts[None, :]) & (positions < seg_ends[None, :])
        membership = member.astype(jnp.bfloat16)
        inside = member[:, :, None]
        normed_one, scale_one = norm_forward(stream_in, gain_one)
        normed_one_low = lower(normed_one)
        self_values = lower(product(normed_one_low, w_self_value, "pd,dc->pc"))
        stream_one = stream_in + head_total(product(self_values, w_self_out, "pc,cd->pd"))
        normed_two, scale_two = norm_forward(stream_one, gain_two)
        normed_two_low = lower(normed_two)
        query_low = lower(product(normed_two_low, w_query, "pd,dc->pc"))
        key_low = lower(product(encoder_rows, w_key, "ed,dc->ec"))
        value_low = lower(product(encoder_rows, w_value, "ed,dc->ec"))
        columns = key_low.shape[1]
        heads_here = columns // HEAD_DIM
        token_query = product(membership, query_low, "ep,pc->ec")
        query_heads = token_query.reshape(tokens, heads_here, HEAD_DIM)
        key_heads = key_low.reshape(tokens, heads_here, HEAD_DIM)
        value_heads = value_low.reshape(tokens, heads_here, HEAD_DIM)
        scores = jnp.sum(query_heads * key_heads, axis=-1)
        highest = jnp.max(jnp.where(inside, scores[:, None, :], -jnp.inf), axis=0)
        shifted = jnp.exp(scores - spread_rows(inside, highest))
        attend = shifted / spread_rows(
            inside, jnp.sum(jnp.where(inside, shifted[:, None, :], 0.0), axis=0)
        )
        weighted = lower(attend[:, :, None] * value_heads).reshape(tokens, columns)
        context_low = lower(product(membership, weighted, "ep,ec->pc"))
        stream_two = stream_one + head_total(product(context_low, w_cross_out, "pc,cd->pd"))
        normed_three, scale_three = norm_forward(stream_two, gain_three)
        normed_three_low = lower(normed_three)
        before = product(normed_three_low, w_ff_in, "pd,df->pf")
        activated, gelu_back = jax.vjp(jax.nn.gelu, before)
        hidden_low = lower(activated)
        stream_out = stream_two + head_total(product(hidden_low, w_ff_out, "pf,fd->pd"))
        outputs.append(stream_out)
        pair_scores = jnp.sum(stream_out * direction, axis=-1)
        slot_table = pair_slot[micro_index]
        own_slots = lax.dynamic_slice_in_dim(slot_table, member_rank * pair_count, pair_count)
        send_order = jnp.argsort(own_slots)
        arrived = lax.all_to_all(
            pair_scores[send_order].reshape(groups, per_peer),
            "dp",
            split_axis=0,
            concat_axis=0,
            tiled=True,
        ).reshape(pair_count)
        inverse = jnp.argsort(slot_table)
        sources = (
            lax.dynamic_slice_in_dim(inverse, member_rank * pair_count, pair_count) // pair_count
        )
        arrival = jnp.argsort(sources * pair_count + local_index)
        placing = jnp.argsort(arrival)
        logits = arrived[placing].reshape(pair_count // CAND, CAND)
        targets = jax.nn.softmax(relevance[micro_index].reshape(pair_count // CAND, CAND), axis=-1)
        grad_logits = loss_weight * (jax.nn.softmax(logits, axis=-1) - targets)
        returned = lax.all_to_all(
            grad_logits.reshape(pair_count)[arrival].reshape(groups, per_peer),
            "dp",
            split_axis=0,
            concat_axis=0,
            tiled=True,
        ).reshape(pair_count)
        grad_scores = returned[jnp.argsort(send_order)]
        grad_out = grad_scores[:, None] * direction
        ff_low = lower(grad_out)
        grad_hidden = product(ff_low, w_ff_out, "pd,fd->pf")
        grad_ff_out = product(hidden_low, ff_low, "pf,pd->fd")
        grad_before = lower(gelu_back(grad_hidden)[0])
        grad_ff_in = product(normed_three_low, grad_before, "pd,pf->df")
        back_three, grad_gain_three = norm_backward(
            stream_two,
            scale_three,
            gain_three,
            head_total(product(grad_before, w_ff_in, "pf,df->pd")),
        )
        grad_two = grad_out + back_three
        cross_low = lower(grad_two)
        grad_context = lower(product(cross_low, w_cross_out, "pd,cd->pc"))
        grad_cross_out = product(context_low, cross_low, "pc,pd->cd")
        grad_weighted = product(membership, grad_context, "ep,pc->ec").reshape(
            tokens, heads_here, HEAD_DIM
        )
        grad_attend = jnp.sum(grad_weighted * value_heads, axis=-1)
        grad_value = lower((grad_weighted * attend[:, :, None]).reshape(tokens, columns))
        row_total = spread_rows(
            inside, jnp.sum(jnp.where(inside, (attend * grad_attend)[:, None, :], 0.0), axis=0)
        )
        grad_scores_tok = attend * (grad_attend - row_total)
        grad_token_query = lower((grad_scores_tok[:, :, None] * key_heads).reshape(tokens, columns))
        grad_key = lower((grad_scores_tok[:, :, None] * query_heads).reshape(tokens, columns))
        grad_query = lower(product(membership, grad_token_query, "ep,ec->pc"))
        grad_w_query = product(normed_two_low, grad_query, "pd,pc->dc")
        grad_w_key = product(encoder_rows, grad_key, "ed,ec->dc")
        grad_w_value = product(encoder_rows, grad_value, "ed,ec->dc")
        key_parts, value_parts = (
            lax.all_to_all(grad_key, "mp", split_axis=0, concat_axis=1, tiled=True),
            lax.all_to_all(grad_value, "mp", split_axis=0, concat_axis=1, tiled=True),
        )
        grad_encoder = product(key_parts, key_full, "ec,dc->ed") + product(
            value_parts, value_full, "ec,dc->ed"
        )
        grads_enc.append(lower(grad_encoder))
        back_two, grad_gain_two = norm_backward(
            stream_one, scale_two, gain_two, head_total(product(grad_query, w_query, "pc,dc->pd"))
        )
        grad_one = grad_two + back_two
        self_low = lower(grad_one)
        grad_self_values = lower(product(self_low, w_self_out, "pd,cd->pc"))
        grad_w_self_out = product(self_values, self_low, "pc,pd->cd")
        grad_w_self_value = product(normed_one_low, grad_self_values, "pd,pc->dc")
        back_one, grad_gain_one = norm_backward(
            stream_in,
            scale_one,
            gain_one,
            head_total(product(grad_self_values, w_self_value, "pc,dc->pd")),
        )
        grads_in.append(grad_one + back_one)
        local_grads = (
            grad_gain_one,
            grad_gain_two,
            grad_gain_three,
            grad_w_self_value,
            grad_w_query,
            grad_w_key,
            grad_w_value,
            grad_ff_in,
            grad_w_self_out,
            grad_cross_out,
            grad_ff_out,
        )
        scattered = (
            lax.psum_scatter(local_grads[0], "dp", scatter_dimension=0, tiled=True),
            lax.psum_scatter(local_grads[1], "dp", scatter_dimension=0, tiled=True),
            lax.psum_scatter(local_grads[2], "dp", scatter_dimension=0, tiled=True),
            lax.psum_scatter(local_grads[3], "dp", scatter_dimension=0, tiled=True),
            lax.psum_scatter(local_grads[4], "dp", scatter_dimension=0, tiled=True),
            lax.psum_scatter(local_grads[5], "dp", scatter_dimension=0, tiled=True),
            lax.psum_scatter(local_grads[6], "dp", scatter_dimension=0, tiled=True),
            lax.psum_scatter(local_grads[7], "dp", scatter_dimension=0, tiled=True),
            lax.psum_scatter(local_grads[8], "dp", scatter_dimension=1, tiled=True),
            lax.psum_scatter(local_grads[9], "dp", scatter_dimension=1, tiled=True),
            lax.psum_scatter(local_grads[10], "dp", scatter_dimension=1, tiled=True),
        )
        totals = scattered if totals is None else jax.tree.map(jnp.add, totals, scattered)
    return (
        jnp.stack(outputs),
        jnp.stack(grads_in),
        jnp.stack(grads_enc),
        totals[0],
        totals[1],
        totals[2],
        totals[3],
        totals[8],
        totals[4],
        totals[5],
        totals[6],
        totals[9],
        totals[7],
        totals[10],
    )


def solution(mesh):
    in_specs = (
        P(None, "dp", None),
        P(None, "dp", None),
        P(None, "dp", None),
        P(),
        P(None, "dp"),
        P(),
        P("dp"),
        P("dp"),
        P("dp"),
        P("dp", "mp"),
        P("mp", "dp"),
        P("dp", "mp"),
        P("dp", "mp"),
        P("dp", "mp"),
        P("mp", "dp"),
        P("dp", "mp"),
        P("mp", "dp"),
    )
    out_specs = (
        P(None, "dp", None),
        P(None, "dp", None),
        P(None, ("dp", "mp"), None),
        P("dp"),
        P("dp"),
        P("dp"),
        P("dp", "mp"),
        P("mp", "dp"),
        P("dp", "mp"),
        P("dp", "mp"),
        P("dp", "mp"),
        P("mp", "dp"),
        P("dp", "mp"),
        P("mp", "dp"),
    )
    return jax.shard_map(shards, mesh=mesh, in_specs=in_specs, out_specs=out_specs, check_vma=False)
```

profile of v0, /device:TPU:0, one launch (start us, length us, event | category | flops | bytes accessed | tf_op | source)
XLA Modules:
  0.0 1218.8 jit_solution(11060638925168028548)
XLA Ops:
  8.1 33.0 %all_gather.53 = bf16[768,192]{1,0:T(8,128)(2,1)S(1)} all-gather(bf16[96,192]{1,0:T(8,128)(2,1)} %param.26), channel_id=1, replica_groups=mesh['dp'=8,'mp'=4] {'dp'}, dimensions={0}, use_global_device_ids=true | all-gather | bytes 331776 | tf_op jit(solution)/shard_map/all_gather | solution.py:64
  46.6 22.3 %all-reduce.13 = (bf16[768]{0:T(1024)(128)(2,1)S(1)}, bf16[768]{0:T(1024)(128)(2,1)S(1)}, bf16[768]{0:T(1024)(128)(2,1)}) all-reduce(bf16[768]{0:T(1024)(128)(2,1)S(1)} %dynamic-update-slice, bf16[768]{0:T(1024)(128)(2,1)S(1)} %dynamic-update-slice.1, bf16[768]{0:T(1024)(128)(2,1)S(1)} %dynamic-update-slice.2), channel_id=1, replica_groups=mesh['dp'=8,'mp'=4] {'dp'}, use_global_device_ids=true, to_apply=%add | all-reduce | flops 2304 | bytes 9216
  69.8 31.1 %all_gather.54 = bf16[192,768]{0,1:T(8,128)(2,1)S(1)} all-gather(bf16[192,96]{0,1:T(8,128)(2,1)S(1)} %copy.99), channel_id=1, replica_groups=mesh['dp'=8,'mp'=4] {'dp'}, dimensions={1}, use_global_device_ids=true | all-gather | bytes 331776 | tf_op jit(solution)/shard_map/all_gather | solution.py:69
  105.3 31.2 %all_gather.57 = bf16[768,192]{1,0:T(8,128)(2,1)S(1)} all-gather(bf16[96,192]{1,0:T(8,128)(2,1)} %param.29), channel_id=1, replica_groups=mesh['dp'=8,'mp'=4] {'dp'}, dimensions={0}, use_global_device_ids=true | all-gather | bytes 331776 | tf_op jit(solution)/shard_map/all_gather | solution.py:66
  136.5 12.4 %fusion.31 = f32[12288,192]{0,1:T(8,128)} fusion(bf16[768,192]{1,0:T(8,128)(2,1)S(1)} %all_gather.57, bf16[2,12288,768]{2,1,0:T(8,128)(2,1)} %param.18), kind=kOutput, calls=%fused_computation.29 | convolution fusion | flops 3628597248 | bytes 28606464 | tf_op jit(solution)/shard_map/ed,dc->ec/dot_general | solution.py:21
  149.0 12.4 %fusion.37 = f32[12288,192]{0,1:T(8,128)} fusion(bf16[768,192]{1,0:T(8,128)(2,1)S(1)} %all_gather.57, bf16[2,12288,768]{2,1,0:T(8,128)(2,1)} %param.18), kind=kOutput, calls=%fused_computation.31 | convolution fusion | flops 3628597248 | bytes 28606464 | tf_op jit(solution)/shard_map/ed,dc->ec/dot_general | solution.py:21
  161.4 31.1 %all_gather.56 = bf16[768,192]{1,0:T(8,128)(2,1)S(1)} all-gather(bf16[96,192]{1,0:T(8,128)(2,1)S(1)} %copy-done.52), channel_id=1, replica_groups=mesh['dp'=8,'mp'=4] {'dp'}, dimensions={0}, use_global_device_ids=true | all-gather | bytes 331776 | tf_op jit(solution)/shard_map/all_gather | solution.py:65
  194.6 33.1 %all_gather.58 = bf16[768,192]{1,0:T(8,128)(2,1)} all-gather(bf16[96,192]{1,0:T(8,128)(2,1)S(1)} %copy-done.53), channel_id=1, replica_groups=mesh['dp'=8,'mp'=4] {'dp'}, dimensions={0}, use_global_device_ids=true | all-gather | bytes 331776 | tf_op jit(solution)/shard_map/all_gather | solution.py:67
  227.7 31.0 %all_gather.59 = bf16[192,768]{0,1:T(8,128)(2,1)S(1)} all-gather(bf16[192,96]{0,1:T(8,128)(2,1)S(1)} %copy.101), channel_id=1, replica_groups=mesh['dp'=8,'mp'=4] {'dp'}, dimensions={1}, use_global_device_ids=true | all-gather | bytes 331776 | tf_op jit(solution)/shard_map/all_gather | solution.py:70
  260.5 10.1 fusion.162
  283.8 13.1 %fusion.50 = (bf16[12288,192]{0,1:T(8,128)(2,1)}, f32[12288,192]{0,1:T(8,128)}) fusion(f32[12288,3]{0,1:T(4,128)} %div.134, bf16[768,192]{1,0:T(8,128)(2,1)S(1)} %copy-done.15, bf16[2,12288,768]{2,1,0:T(8,128)(2,1)} %param.18), kind=kOutput, calls=%fused_computation.50 | convolution fusion | flops 3633315840 | bytes 33521664 | tf_op jit(solution)/shard_map/ed,dc->ec/dot_general | solution.py:21
  301.5 10.4 fusion.163
  325.1 13.0 %fusion.48 = (bf16[12288,192]{0,1:T(8,128)(2,1)}, f32[12288,192]{0,1:T(8,128)}) fusion(f32[12288,3]{0,1:T(4,128)} %div.130, bf16[768,192]{1,0:T(8,128)(2,1)S(1)} %copy-done.15, bf16[2,12288,768]{2,1,0:T(8,128)(2,1)} %param.18), kind=kOutput, calls=%fused_computation.48 | convolution fusion | flops 3633315840 | bytes 33521664 | tf_op jit(solution)/shard_map/ed,dc->ec/dot_general | solution.py:21
  387.6 40.5 %all-gather.7.cloned.1.call-done = bf16[768,768]{0,1:T(8,128)(2,1)} async-done(((bf16[768,96]{0,1:T(8,128)(2,1)}), bf16[768,768]{0,1:T(8,128)(2,1)}) %all-gather.7.cloned.1.call-update) | async-done | bytes 1179664 | tf_op jit(solution)/shard_map/all_gather | solution.py:71
  436.6 30.2 %all-reduce.27.cloned.1.call-done = (f32[64,768]{1,0:T(8,128)}, f32[64,768]{1,0:T(8,128)}) async-done(((f32[64,768]{1,0:T(8,128)}, f32[64,768]{1,0:T(8,128)}), (f32[64,768]{1,0:T(8,128)}, f32[64,768]{1,0:T(8,128)})) %all-reduce.27.cloned.1.call-update) | async-done | bytes 393232 | tf_op jit(solution)/shard_map/psum | solution.py:40
  543.0 30.1 %all-reduce.25.cloned.1.call-done = (f32[64,768]{1,0:T(8,128)}, f32[64,768]{1,0:T(8,128)}) async-done(((f32[64,768]{1,0:T(8,128)}, f32[64,768]{1,0:T(8,128)}), (f32[64,768]{1,0:T(8,128)}, f32[64,768]{1,0:T(8,128)})) %all-reduce.25.cloned.1.call-update) | async-done | bytes 393232 | tf_op jit(solution)/shard_map/psum | solution.py:40
  633.5 32.6 %all-reduce.23.cloned.1.call-done = (f32[64,768]{1,0:T(8,128)}, f32[64,768]{1,0:T(8,128)}) async-done(((f32[64,768]{1,0:T(8,128)}, f32[64,768]{1,0:T(8,128)}), (f32[64,768]{1,0:T(8,128)}, f32[64,768]{1,0:T(8,128)})) %all-reduce.23.cloned.1.call-update) | async-done | bytes 393232 | tf_op jit(solution)/shard_map/psum | solution.py:40
  689.9 10.1 fusion.2
  700.0 10.0 fusion.63
  711.3 10.2 fusion
  721.5 10.0 fusion.69
  737.6 20.8 %all-to-all-done.6 = bf16[4,3072,192]{1,2,0:T(8,128)(2,1)} async-done(((bf16[4,3072,192]{1,2,0:T(8,128)(2,1)}), bf16[4,3072,192]{1,2,0:T(8,128)(2,1)}, u32[]{:S(2)}, u32[]{:S(2)}) %all-to-all-start.6) | async-done | bytes 4718624 | tf_op jit(solution)/shard_map/all_to_all | solution.py:245
  773.1 44.3 %all-to-all-done.7 = bf16[4,3072,192]{1,2,0:T(8,128)(2,1)} async-done(((bf16[4,3072,192]{1,2,0:T(8,128)(2,1)}), bf16[4,3072,192]{1,2,0:T(8,128)(2,1)}, u32[]{:S(2)}, u32[]{:S(2)}) %all-to-all-start.7) | async-done | bytes 4718624 | tf_op jit(solution)/shard_map/all_to_all | solution.py:246
  833.1 43.3 %all-to-all-done.4 = bf16[4,3072,192]{1,2,0:T(8,128)(2,1)} async-done(((bf16[4,3072,192]{1,2,0:T(8,128)(2,1)}), bf16[4,3072,192]{1,2,0:T(8,128)(2,1)}, u32[]{:S(2)}, u32[]{:S(2)}) %all-to-all-start.4) | async-done | bytes 4718624 | tf_op jit(solution)/shard_map/all_to_all | solution.py:245
  881.7 37.5 %all-reduce.6 = (f32[768]{0:T(1024)S(1)}, f32[768]{0:T(1024)S(1)}, f32[768]{0:T(1024)S(1)}) all-reduce(f32[768]{0:T(1024)S(1)} %add.289, f32[768]{0:T(1024)S(1)} %add.290, f32[768]{0:T(1024)S(1)} %add.291), channel_id=13, replica_groups=mesh['dp'=8,'mp'=4] {'dp'}, use_global_device_ids=true, to_apply=%region_63.64.clone | all-reduce | flops 2304 | bytes 18432
  925.1 10.4 fusion.179
  944.1 11.7 fusion.57
  955.8 10.1 fusion.56
  974.4 27.0 %reduce-scatter.29.cloned.1.call-done = f32[96,192]{1,0:T(8,128)} async-done(((f32[768,192]{1,0:T(8,128)}), f32[96,192]{1,0:T(8,128)}) %reduce-scatter.29.cloned.1.call-update) | async-done | bytes 73744
  1001.3 65.7 %reduce-scatter.17.cloned.1.call-done = f32[96,192]{1,0:T(8,128)} async-done(((f32[768,192]{1,0:T(8,128)}), f32[96,192]{1,0:T(8,128)}) %reduce-scatter.17.cloned.1.call-update) | async-done | bytes 73744 | tf_op jit(solution)/shard_map/reduce_scatter | solution.py:284
  1067.0 72.0 %reduce-scatter.21.cloned.1.call-done = f32[96,768]{1,0:T(8,128)} async-done(((f32[768,768]{1,0:T(8,128)}), f32[96,768]{1,0:T(8,128)}) %reduce-scatter.21.cloned.1.call-update) | async-done | bytes 294928 | tf_op jit(solution)/shard_map/reduce_scatter | solution.py:288
  1139.0 72.2 %reduce-scatter.23.cloned.1.call-done = f32[768,96]{0,1:T(8,128)} async-done(((f32[768,768]{0,1:T(8,128)}), f32[768,96]{0,1:T(8,128)}) %reduce-scatter.23.cloned.1.call-update) | async-done | bytes 294928 | tf_op jit(solution)/shard_map/reduce_scatter | solution.py:291
  (474 shorter events, 327.6 us)
Async XLA Ops:
  8.0 250.6 %all-reduce.31.cloned.1.call-start = ((), (), s32[]{:S(2)}) async-start(), calls=%async_computation.33 | async-start | bytes 786432 | tf_op jit(solution)/shard_map/psum | solution.py:40
  105.3 271.3 %all-reduce.29.cloned.1.call-start = ((), (), s32[]{:S(2)}) async-start(), calls=%async_computation.32 | async-start | bytes 786432 | tf_op jit(solution)/shard_map/psum | solution.py:40
  149.0 109.6 %copy-start.9 = (bf16[2,64,768]{2,1,0:T(8,128)(2,1)S(1)}, bf16[2,64,768]{2,1,0:T(8,128)(2,1)}, u32[]{:S(2)}) copy-start(bf16[2,64,768]{2,1,0:T(8,128)(2,1)} %param.17) | copy-start | bytes 589828
  193.1 145.0 %copy-start.59 = (s32[64]{0:T(128)}, s32[64]{0:T(128)S(1)}, u32[]{:S(2)}) copy-start(s32[64]{0:T(128)S(1)} %reduce) | copy-start | bytes 772
  193.2 144.9 %copy-start.68 = (s32[64]{0:T(128)}, s32[64]{0:T(128)S(1)}, u32[]{:S(2)}) copy-start(s32[64]{0:T(128)S(1)} %get-tuple-element.173) | copy-start | bytes 772
  260.5 116.1 %copy-start.7 = (f32[64,768]{1,0:T(8,128)}, f32[64,768]{1,0:T(8,128)S(1)}, u32[]{:S(2)}) copy-start(f32[64,768]{1,0:T(8,128)S(1)} %get-tuple-element.163) | copy-start | bytes 589828
  260.5 117.2 %copy-start.5 = (f32[64,768]{1,0:T(8,128)}, f32[64,768]{1,0:T(8,128)S(1)}, u32[]{:S(2)}) copy-start(f32[64,768]{1,0:T(8,128)S(1)} %get-tuple-element.147) | copy-start | bytes 589828
  344.1 41.9 %all-gather.5.cloned.1.call-start = ((), (), s32[]{:S(2)}) async-start(), calls=%async_computation.16 | async-start | bytes 1327104 | tf_op jit(solution)/shard_map/all_gather | solution.py:68
  344.7 83.4 %all-gather.7.cloned.1.call-start = ((), (), s32[]{:S(2)}) async-start(), calls=%async_computation.17 | async-start | bytes 1327104 | tf_op jit(solution)/shard_map/all_gather | solution.py:71
  345.3 121.6 %all-reduce.27.cloned.1.call-start = ((), (), s32[]{:S(2)}) async-start(), calls=%async_computation.31 | async-start | bytes 786432 | tf_op jit(solution)/shard_map/psum | solution.py:40
  432.9 105.3 %copy-start = (bf16[768,768]{1,0:T(8,128)(2,1)S(1)}, bf16[768,768]{1,0:T(8,128)(2,1)}, u32[]{:S(2)}) copy-start(bf16[768,768]{1,0:T(8,128)(2,1)} %all-gather.5.cloned.1.call-done) | copy-start | bytes 3538948
  471.7 15.9 %all-to-all-start = ((f32[8,1,8]{2,1,0:T(1,128)}), f32[8,1,8]{2,1,0:T(1,128)S(1)}, u32[]{:S(2)}, u32[]{:S(2)}) async-start(f32[8,1,8]{2,1,0:T(1,128)} %bitcast.266), calls=%async_computation | async-start | bytes 8192 | tf_op jit(solution)/shard_map/all_to_all | solution.py:189
  487.6 12.4 %all-to-all-start.2 = ((f32[8,1,8]{2,1,0:T(1,128)}), f32[8,1,8]{2,1,0:T(1,128)}, u32[]{:S(2)}, u32[]{:S(2)}) async-start(f32[8,1,8]{2,1,0:T(1,128)} %bitcast.26), calls=%async_computation.2 | async-start | bytes 8192 | tf_op jit(solution)/shard_map/all_to_all | solution.py:189
  508.2 11.7 all-to-all-start.3
  519.9 10.3 all-to-all-start.1
  523.8 49.3 %all-reduce.25.cloned.1.call-start = ((), (), s32[]{:S(2)}) async-start(), calls=%async_computation.30 | async-start | bytes 786432 | tf_op jit(solution)/shard_map/psum | solution.py:40
  542.9 123.2 %all-reduce.23.cloned.1.call-start = ((), (), s32[]{:S(2)}) async-start(), calls=%async_computation.29 | async-start | bytes 786432 | tf_op jit(solution)/shard_map/psum | solution.py:40
  633.2 198.6 %all-reduce.21.cloned.1.call-start = ((), (), s32[]{:S(2)}) async-start(), calls=%async_computation.28 | async-start | bytes 786432 | tf_op jit(solution)/shard_map/psum | solution.py:40
  672.9 248.9 %reduce-scatter.31.cloned.1.call-start = ((), (), s32[]{:S(2)}) async-start(), calls=%async_computation.27 | async-start | bytes 884736
  674.5 249.0 %reduce-scatter.25.cloned.1.call-start = ((), (), s32[]{:S(2)}) async-start(), calls=%async_computation.24 | async-start | bytes 884736
  676.3 248.8 %all-gather.9.cloned.1.call-start = ((), (), s32[]{:S(2)}) async-start(), calls=%async_computation.18 | async-start | bytes 1474560 | tf_op jit(solution)/shard_map/all_gather | solution.py:74
  677.2 266.9 %all-gather.11.cloned.1.call-start = ((), (), s32[]{:S(2)}) async-start(), calls=%async_computation.19 | async-start | bytes 1474560 | tf_op jit(solution)/shard_map/all_gather | solution.py:75
  683.5 74.8 %all-to-all-start.6 = ((bf16[4,3072,192]{1,2,0:T(8,128)(2,1)}), bf16[4,3072,192]{1,2,0:T(8,128)(2,1)}, u32[]{:S(2)}, u32[]{:S(2)}) async-start(bf16[4,3072,192]{1,2,0:T(8,128)(2,1)} %bitcast.258), calls=%async_computation.6 | async-start | bytes 9437184 | tf_op jit(solution)/shard_map/all_to_all | solution.py:245
  688.6 285.8 %reduce-scatter.19.cloned.1.call-start = ((), (), s32[]{:S(2)}) async-start(), calls=%async_computation.21 | async-start | bytes 884736 | tf_op jit(solution)/shard_map/reduce_scatter | solution.py:285
  700.0 274.4 %reduce-scatter.27.cloned.1.call-start = ((), (), s32[]{:S(2)}) async-start(), calls=%async_computation.25 | async-start | bytes 884736
  711.2 290.1 %reduce-scatter.29.cloned.1.call-start = ((), (), s32[]{:S(2)}) async-start(), calls=%async_computation.26 | async-start | bytes 884736
  758.4 58.9 %all-to-all-start.7 = ((bf16[4,3072,192]{1,2,0:T(8,128)(2,1)}), bf16[4,3072,192]{1,2,0:T(8,128)(2,1)}, u32[]{:S(2)}, u32[]{:S(2)}) async-start(bf16[4,3072,192]{1,2,0:T(8,128)(2,1)} %bitcast.259), calls=%async_computation.7 | async-start | bytes 9437184 | tf_op jit(solution)/shard_map/all_to_all | solution.py:246
  763.6 303.4 %reduce-scatter.17.cloned.1.call-start = ((), (), s32[]{:S(2)}) async-start(), calls=%async_computation.20 | async-start | bytes 884736 | tf_op jit(solution)/shard_map/reduce_scatter | solution.py:284
  765.3 373.7 %reduce-scatter.21.cloned.1.call-start = ((), (), s32[]{:S(2)}) async-start(), calls=%async_computation.22 | async-start | bytes 2654208 | tf_op jit(solution)/shard_map/reduce_scatter | solution.py:288
  817.4 59.0 %all-to-all-start.4 = ((bf16[4,3072,192]{1,2,0:T(8,128)(2,1)}), bf16[4,3072,192]{1,2,0:T(8,128)(2,1)}, u32[]{:S(2)}, u32[]{:S(2)}) async-start(bf16[4,3072,192]{1,2,0:T(8,128)(2,1)} %bitcast.257), calls=%async_computation.4 | async-start | bytes 9437184 | tf_op jit(solution)/shard_map/all_to_all | solution.py:245
  822.5 388.7 %reduce-scatter.23.cloned.1.call-start = ((), (), s32[]{:S(2)}) async-start(), calls=%async_computation.23 | async-start | bytes 2654208 | tf_op jit(solution)/shard_map/reduce_scatter | solution.py:291
  876.4 79.4 %all-to-all-start.5 = ((bf16[4,3072,192]{1,2,0:T(8,128)(2,1)}), bf16[4,3072,192]{1,2,0:T(8,128)(2,1)}, u32[]{:S(2)}, u32[]{:S(2)}) async-start(bf16[4,3072,192]{1,2,0:T(8,128)(2,1)} %bitcast.256), calls=%async_computation.5 | async-start | bytes 9437184 | tf_op jit(solution)/shard_map/all_to_all | solution.py:246
  (91 other events, 1683.2 us)
Sparse Core Ops, SparseCore 0:
  105.4 29.9 all-reduce.30
  344.2 30.1 all-reduce.28
  435.6 31.1 all-reduce.26
  543.0 29.9 all-reduce.24
  633.3 32.7 all-reduce.22
  673.0 33.6 all-reduce.20
  708.3 23.9 all-gather.8
  733.8 23.8 all-gather.10
Sparse Core Ops, SparseCore 1:
  346.8 39.2 all-gather.4
  388.0 40.0 all-gather.6
  676.7 62.6 reduce-scatter.30
  743.0 61.6 reduce-scatter.24
  808.6 61.6 reduce-scatter.18
  874.4 61.6 reduce-scatter.26
  939.8 61.5 reduce-scatter.28
  1005.4 61.5 reduce-scatter.16
  1070.9 68.0 reduce-scatter.20
  1143.1 68.0 reduce-scatter.22
where the time goes:
time: 1230 us; the launch traced here: 1220 us
  waiting for transfers between devices  493 us (40%)
  blocking collectives  250 us (20%)
  matrix products  216 us (18%)
  other arithmetic  129 us (10%)
  local copies, waits for them, and re-layouts  70.2 us (6%)
  starting transfers between devices  41.9 us (3%)
  between operations  18.6 us (2%)
    dot_general x52, matrix products, product(): return jnp.einsum(form, left, right, preferred_element_type=jnp.float32)  216 us
    psum x6, waiting for transfers between devices, head_total(): return lax.psum(partial_value, 'mp')  92.9 us
    reduce_scatter x1, waiting for transfers between devices, shards(): lax.psum_scatter(local_grads[10], 'dp', scatter_dimension=1, tiled=True)  72.2 us
    reduce_scatter x1, waiting for transfers between devices, shards(): lax.psum_scatter(local_grads[7], 'dp', scatter_dimension=0, tiled=True)  72 us
    reduce_scatter x1, waiting for transfers between devices, shards(): lax.psum_scatter(local_grads[3], 'dp', scatter_dimension=0, tiled=True)  65.7 us
    all_to_all x2, waiting for transfers between devices, shards(): lax.all_to_all(grad_key, 'mp', split_axis=0, concat_axis=1, tiled=True)  64 us
    unnamed x2, blocking collectives  59.8 us
    all_to_all x2, waiting for transfers between devices, shards(): lax.all_to_all(grad_value, 'mp', split_axis=0, concat_axis=1, tiled=True)  44.3 us
  transfers between devices with their start and end apart: 26, of which 15 were waited for; matrix products, arithmetic and copies ran while one was open for 18% of the time, Pallas kernels for 0%

commit v1 on v0

v1 whole, which is shorter than its diff:
```python
import functools
import math

import jax
import jax.numpy as jnp
from jax import lax
from jax.experimental import pallas as pl
from jax.experimental.pallas import tpu as pltpu
from jax.sharding import PartitionSpec as P

MESH = pl.DeviceIdType.MESH
CAND = 16

def when(cond, fn):
    if isinstance(cond, bool):
        if cond: fn()
    else:
        pl.when(cond)(fn)

def gather_kernel(groups, rows_a, a_ref, b_ref, oa, ob, own, za, zb, ya, yb, xa, ca, ra, rb):
    lines = groups // 2
    d = lax.axis_index("dp")
    m = lax.axis_index("mp")
    o, i = d // 2, d % 2
    xm, cm = (m + 2) % 4, m + 1 - 2 * (m % 2)
    xcm = (cm + 2) % 4
    def dev(dd, mm):
        return (dd, mm)
    barrier = pltpu.get_barrier_semaphore()
    def hello(dd, mm):
        pl.semaphore_signal(barrier, inc=1, device_id=(dd, mm), device_id_type=MESH)
    hello(d + 1 - 2 * i, m); hello(d, xm); hello(d, cm)
    pl.when(o + 1 < lines)(lambda: hello(d + 2, m))
    pl.when(o > 0)(lambda: hello(d - 2, m))
    count = 3 + jnp.where(o + 1 < lines, 1, 0) + jnp.where(o > 0, 1, 0)
    pl.semaphore_wait(barrier, count)
    def put(src, dst, ssem, rsem, dd, mm):
        return pltpu.make_async_remote_copy(src_ref=src, dst_ref=dst, send_sem=ssem, recv_sem=rsem, device_id=(dd, mm), device_id_type=MESH)
    def a_at(mm, dd): return oa.at[mm, dd]
    def b_at(dd): return ob.at[dd]
    def send_a(dd, src, right, left, y, which_x, core):
        pass
    def right(dd, src_a, src_b):
        def go():
            put(src_a, a_at(m, dd), za.at[0, dd], ra.at[m, dd], d + 2, m).start()
            put(src_b, b_at(dd), zb.at[0, dd], rb.at[dd], d + 2, m).start()
        pl.when(o + 1 < lines)(go)
    def left(dd, src_a, src_b):
        def go():
            put(src_a, a_at(m, dd), za.at[1, dd], ra.at[m, dd], d - 2, m).start()
            put(src_b, b_at(dd), zb.at[1, dd], rb.at[dd], d - 2, m).start()
        pl.when(o > 0)(go)
    def yput(dd, src_a, src_b):
        put(src_a, a_at(m, dd), ya.at[dd], ra.at[m, dd], d + 1 - 2 * i, m).start()
        put(src_b, b_at(dd), yb.at[dd], rb.at[dd], d + 1 - 2 * i, m).start()
    def mates(dd, src_a):
        put(src_a, a_at(m, dd), xa.at[dd], ra.at[m, dd], d, xm).start()
        put(src_a, a_at(m, dd), ca.at[0, dd], ra.at[m, dd], d, cm).start()
    def got_a(mm, dd):
        put(a_at(mm, dd), a_at(mm, dd), xa.at[dd], ra.at[mm, dd], d, xm).wait_recv()
    def got_b(dd):
        put(b_at(dd), b_at(dd), yb.at[dd], rb.at[dd], d, xm).wait_recv()
    def from_x(dd):
        got_a(xm, dd)
        put(a_at(xm, dd), a_at(xm, dd), ca.at[1, dd], ra.at[xm, dd], d, cm).start()
    keep_a = pltpu.make_async_copy(a_ref, a_at(m, d), own.at[0])
    keep_b = pltpu.make_async_copy(b_ref, b_at(d), own.at[1])
    right(d, a_ref, b_ref); left(d, a_ref, b_ref); yput(d, a_ref, b_ref); mates(d, a_ref)
    keep_a.start(); keep_b.start()
    for k in range(1, lines):
        def west(k=k):
            dd = d - 2 * k
            got_a(m, dd); got_b(dd)
            right(dd, a_at(m, dd), b_at(dd)); yput(dd, a_at(m, dd), b_at(dd)); mates(dd, a_at(m, dd))
        pl.when(o - k >= 0)(west)
        def east(k=k):
            dd = d + 2 * k
            got_a(m, dd); got_b(dd)
            left(dd, a_at(m, dd), b_at(dd)); yput(dd, a_at(m, dd), b_at(dd)); mates(dd, a_at(m, dd))
        pl.when(o + k < lines)(east)
        if k == 1:
            from_x(d)
        else:
            pl.when(o - (k - 1) >= 0)(lambda k=k: from_x(d - 2 * (k - 1)))
            pl.when(o + (k - 1) < lines)(lambda k=k: from_x(d + 2 * (k - 1)))
    pl.when(o - (lines - 1) >= 0)(lambda: from_x(d - 2 * (lines - 1)))
    pl.when(o + (lines - 1) < lines)(lambda: from_x(d + 2 * (lines - 1)))
    dy = d + 1 - 2 * i
    def across(dd):
        got_a(m, dd); got_b(dd)
        mates(dd, a_at(m, dd))
    def order(fn, base):
        fn(base)
        for k in range(1, lines):
            pl.when(o - k >= 0)(lambda k=k: fn(base - 2 * k))
            pl.when(o + k < lines)(lambda k=k: fn(base + 2 * k))
    order(across, dy)
    order(from_x, dy)
    for dd in range(groups):
        got_a(cm, dd); got_a(xcm, dd)
    keep_a.wait(); keep_b.wait()
    def sent(src, sem):
        put(src, src, sem, ra.at[0, 0], d, xm).wait_send()
    for dd in range(groups):
        sent(a_at(m, dd), xa.at[dd]); sent(a_at(m, dd), ca.at[0, dd]); sent(a_at(m, dd), ca.at[1, dd])
    def line_sends(dd, oo):
        def r():
            sent(a_at(m, dd), za.at[0, dd]); sent(b_at(dd), zb.at[0, dd])
        def l():
            sent(a_at(m, dd), za.at[1, dd]); sent(b_at(dd), zb.at[1, dd])
        pl.when((oo <= o) & (o + 1 < lines))(r)
        pl.when((oo >= o) & (o > 0))(l)
        sent(a_at(m, dd), ya.at[dd]); sent(b_at(dd), yb.at[dd])
    for oo in range(lines):
        line_sends(oo * 2 + i, oo)

def gather(groups, a, b):
    ra, ca_ = a.shape
    out = (jax.ShapeDtypeStruct((4, groups) + a.shape, a.dtype), jax.ShapeDtypeStruct((groups,) + b.shape, b.dtype))
    S = pltpu.SemaphoreType.DMA
    return pl.pallas_call(functools.partial(gather_kernel, groups, ra), out_shape=out,
        in_specs=[pl.BlockSpec(memory_space=pl.ANY)] * 2, out_specs=[pl.BlockSpec(memory_space=pl.ANY)] * 2,
        scratch_shapes=[S((2,)), S((2, groups)), S((2, groups)), S((groups,)), S((groups,)), S((groups,)), S((2, groups)), S((4, groups)), S((groups,))],
        compiler_params=pltpu.CompilerParams(collective_id=0, has_side_effects=True), name="gather_weights")(a, b)

bf16, f32 = jnp.bfloat16, jnp.float32
D, HEAD, HEADS = 768, 64, 12
PER = HEADS // 4
WIN = 8
TILE = 256
eps = 1e-6
FAR = -1e30
VMEM = 60 << 20

def dot(a, b, ca=1, cb=0):
    return lax.dot_general(a, b, (((ca,), (cb,)), ((), ())), preferred_element_type=f32)

def exact(a, b):
    return lax.dot_general(a, b, (((1,), (0,)), ((), ())), preferred_element_type=f32, precision=lax.Precision.HIGHEST)

def rms(v):
    r = lax.rsqrt(jnp.mean(v * v, axis=-1, keepdims=True) + eps)
    return v * r, r

def head_of(shape, axis):
    return lax.broadcasted_iota(jnp.int32, shape, axis) // WIN

def expand(x):
    col = lax.broadcasted_iota(jnp.int32, x.shape, 1) // HEAD
    return jnp.concatenate([jnp.where(col == j, x, 0) for j in range(PER)], axis=0)

def collapse(x, rows):
    out = 0
    for j in range(PER):
        part = x[j * rows:(j + 1) * rows]
        col = lax.broadcasted_iota(jnp.int32, part.shape, 1) // HEAD
        out = out + jnp.where(col == j, part, 0)
    return out

def per_head(x, m, rows):
    col = lax.broadcasted_iota(jnp.int32, (rows, PER * HEAD), 1) // HEAD
    out = x[:, PER * m:PER * m + 1]
    out = jnp.where(col == 0, out, 0)
    for j in range(1, PER):
        out = jnp.where(col == j, x[:, PER * m + j:PER * m + j + 1], out)
    return out

def to_pairs(x):
    n = x.shape[0]
    wide = jnp.broadcast_to(x[:, None, :], (n, WIN, 128)).reshape(n * WIN, 128)
    lane = lax.broadcasted_iota(jnp.int32, wide.shape, 1)
    row = lax.broadcasted_iota(jnp.int32, wide.shape, 0)
    wide = jnp.where(lane % WIN == row % WIN, wide, 0.0)
    pick = (head_of((128, 128), 0) == lax.broadcasted_iota(jnp.int32, (128, 128), 1)).astype(f32)
    return exact(wide, pick)

def to_windows(x):
    pick = (lax.broadcasted_iota(jnp.int32, (128, 128), 0) == head_of((128, 128), 1)).astype(f32)
    wide = exact(x, pick)
    lane = lax.broadcasted_iota(jnp.int32, wide.shape, 1)
    row = lax.broadcasted_iota(jnp.int32, wide.shape, 0)
    wide = jnp.where(lane % WIN == row % WIN, wide, 0.0)
    return jnp.sum(wide.reshape(-1, WIN, 128), axis=1)

SV, SO, WQ, WK, WV, CO = 0, 192, 384, 576, 768, 960

def fill_windows(stage, m, rows, pairs):
    micro = stage.shape[0]
    n = micro * pairs
    for j in range(PER):
        h = PER * m + j
        stage[:, :, h * WIN:(h + 1) * WIN, :] = rows[j * n:(j + 1) * n].reshape(micro, pairs // WIN, WIN, D)

def front_kernel(micros, pairs, tiles, rank_ref, wlo, whi, x0_ref, a_hbm, enc_hbm, lo_ref, hi_ref,
                 x1_ref, v1_ref, q_ref, qk_ref, p_ref, c_ref, mx_ref, ctx_ref, lse_ref,
                 w_ref, enc, stage, s_scr, m_scr, l_scr, wsem, esem):
    wins = pairs // WIN
    span = tiles * TILE
    wcopy = pltpu.make_async_copy(a_hbm.at[:, :, 0:1024], w_ref, wsem)
    wcopy.start()
    base = rank_ref[0] * span
    def piece(u, t):
        return pltpu.make_async_copy(enc_hbm.at[u, pl.ds(pl.multiple_of(base + t * TILE, TILE), TILE), :],
                                     enc.at[u, pl.ds(t * TILE, TILE), :], esem.at[u, t])
    for u in range(micros):
        for t in range(tiles):
            piece(u, t).start()
    x0 = x0_ref[...].astype(f32)
    y1 = rms(x0)[0].astype(bf16)
    stage[:, :, HEADS * WIN:, :] = jnp.zeros((micros, wins, 128 - HEADS * WIN, D), f32)
    wcopy.wait()
    x1 = x0
    for m in range(4):
        v1 = dot(y1, w_ref[m, :, SV:SV + 192]).astype(bf16)
        v1_ref[m] = v1
        x1 = x1 + dot(v1, w_ref[m, :, SO:SO + 192], 1, 1)
    x1_ref[...] = x1
    y2 = rms(x1)[0].astype(bf16)
    for m in range(4):
        q = dot(y2, w_ref[m, :, WQ:WQ + 192]).astype(bf16)
        q_ref[m] = q
        fill_windows(stage, m, dot(expand(q), w_ref[m, :, WK:WK + 192], 1, 1), pairs)
    qk_ref[...] = stage[...].astype(bf16)
    stage[...] = jnp.zeros_like(stage)
    m_scr[...] = jnp.full(m_scr.shape, FAR, f32)
    l_scr[...] = jnp.zeros_like(l_scr)
    for u in range(micros):
        def first(t, _, u=u):
            piece(u, t).wait()
            rows = enc[u, pl.ds(pl.multiple_of(t * TILE, TILE), TILE), :]
            at = base + t * TILE + lax.broadcasted_iota(jnp.int32, (TILE, 128), 0)
            def block(w, _):
                s = dot(rows, qk_ref[u, w], 1, 1)
                s = jnp.where((at >= lo_ref[u, w]) & (at < hi_ref[u, w]), s, FAR)
                s_scr[t + w - wlo[u, 0]] = s
                m_scr[u, w] = jnp.maximum(m_scr[u, w], jnp.max(s, axis=0, keepdims=True))
                return 0
            return lax.fori_loop(wlo[u, t], whi[u, t] + 1, block, 0)
        lax.fori_loop(0, tiles, first, 0)
        def second(t, _, u=u):
            rows = enc[u, pl.ds(pl.multiple_of(t * TILE, TILE), TILE), :]
            def block(w, _):
                k = t + w - wlo[u, 0]
                s = s_scr[k]
                p = jnp.where(s > FAR, jnp.exp(s - m_scr[u, w]), 0.0)
                l_scr[u, w] = l_scr[u, w] + jnp.sum(p, axis=0, keepdims=True)
                low = p.astype(bf16)
                p_ref[u, k] = low
                stage[u, w] = stage[u, w] + dot(low, rows, 0, 0)
                return 0
            return lax.fori_loop(wlo[u, t], whi[u, t] + 1, block, 0)
        lax.fori_loop(0, tiles, second, 0)
    n = micros * pairs
    mx = to_pairs(m_scr[...].reshape(micros * wins, 128))
    lx = to_pairs(l_scr[...].reshape(micros * wins, 128))
    some = lx > 0.0
    inv = jnp.where(some, 1.0 / jnp.where(some, lx, 1.0), 0.0)
    mx_ref[...] = mx
    lse_ref[...] = jnp.where(some, mx + jnp.log(jnp.where(some, lx, 1.0)), FAR)
    for h in range(HEADS):
        rows = stage[:, :, h * WIN:(h + 1) * WIN, :].reshape(n, D) * inv[:, h:h + 1]
        c_ref[h] = rows.astype(bf16)
    for m in range(4):
        rows = c_ref[PER * m:PER * (m + 1)].reshape(PER * n, D)
        ctx_ref[m] = collapse(dot(rows, w_ref[m, :, WV:WV + 192]), n).astype(bf16)

def front(rank, wlo, whi, x0, a_full, encoded, lo, hi):
    micros, pairs = encoded.shape[0], x0.shape[0] // encoded.shape[0]
    tiles = wlo.shape[1]
    wins = pairs // WIN
    n = micros * pairs
    steps = tiles + wins - 1
    sd = jax.ShapeDtypeStruct
    any_, vm, sm = (pl.BlockSpec(memory_space=s) for s in (pl.ANY, pltpu.VMEM, pltpu.SMEM))
    return pl.pallas_call(
        functools.partial(front_kernel, micros, pairs, tiles),
        out_shape=(sd((n, D), f32), sd((4, n, 192), bf16), sd((4, n, 192), bf16), sd((micros, wins, 128, D), bf16),
                   sd((micros, steps, TILE, 128), bf16), sd((HEADS, n, D), bf16), sd((n, 128), f32), sd((4, n, 192), bf16), sd((n, 128), f32)),
        in_specs=[sm, sm, sm, vm, any_, any_, vm, vm],
        out_specs=[vm] * 9,
        scratch_shapes=[pltpu.VMEM((4, D, 1024), bf16), pltpu.VMEM((micros, tiles * TILE, D), bf16),
                        pltpu.VMEM((micros, wins, 128, D), f32), pltpu.VMEM((steps, TILE, 128), f32),
                        pltpu.VMEM((micros, wins, 1, 128), f32), pltpu.VMEM((micros, wins, 1, 128), f32),
                        pltpu.SemaphoreType.DMA, pltpu.SemaphoreType.DMA((micros, tiles))],
        compiler_params=pltpu.CompilerParams(vmem_limit_bytes=VMEM),
        name="attention_forward",
    )(rank, wlo, whi, x0, a_full, encoded, lo, hi)

def back_kernel(micros, pairs, tiles, rank_ref, wlo, whi, enc_ref, a_hbm, qk_ref, p_ref, c_ref, mx_ref, lse_loc, lse_ref, delta_ref, dctx_ref, q_ref,
                de_ref, dq_ref, gkv_ref, w_ref, stage, qu, alpha, delta, acc, wsem):
    wins = pairs // WIN
    n = micros * pairs
    g = pl.program_id(0)
    u, t = g // tiles, g % tiles
    wcopy = pltpu.make_async_copy(a_hbm.at[:, :, 512:1024], w_ref, wsem)
    @pl.when(g == 0)
    def _():
        wcopy.start()
        lse = lse_ref[...]
        alpha[...] = to_windows(jnp.exp(jnp.minimum(mx_ref[...] - lse, 1.0))).reshape(alpha.shape)
        delta[...] = to_windows(delta_ref[...]).reshape(delta.shape)
        qu[:, :, 0:128, :] = qk_ref[...]
        stage[:, :, HEADS * WIN:, :] = jnp.zeros((micros, wins, 128 - HEADS * WIN, D), f32)
        share = jnp.exp(jnp.minimum(lse_loc[...] - lse, 1.0))
        wcopy.wait()
        for m in range(4):
            dctx = expand(dctx_ref[m])
            fill_windows(stage, m, dot(dctx, w_ref[m, :, 256:448], 1, 1), pairs)
            scaled = jnp.concatenate([dctx[j * n:(j + 1) * n] * share[:, PER * m + j:PER * m + j + 1].astype(bf16) for j in range(PER)], axis=0)
            gkv_ref[m, :, 192:384] = dot(c_ref[PER * m:PER * (m + 1)].reshape(PER * n, D), scaled, 0, 0).astype(bf16)
        qu[:, :, 128:256, :] = stage[...].astype(bf16)
        stage[...] = jnp.zeros_like(stage)
    rows = enc_ref[0]
    first = wlo[u, t]
    def block(w):
        da = dot(rows, qu[u, w, 128:256, :], 1, 1)
        a = p_ref[u, t + w - wlo[u, 0]].astype(f32) * alpha[u, w]
        ds = a * (da - delta[u, w])
        both = jnp.concatenate([ds.astype(bf16), a.astype(bf16)], axis=1)
        stage[u, w] = stage[u, w] + dot(both[:, 0:128], rows, 0, 0)
        return dot(both, qu[u, w])
    acc[...] = block(first)
    def more(w, _):
        acc[...] = acc[...] + block(w)
        return 0
    lax.fori_loop(first + 1, whi[u, t] + 1, more, 0)
    de_ref[0] = acc[...].astype(bf16)
    @pl.when(g == micros * tiles - 1)
    def _():
        for m in range(4):
            e = jnp.concatenate([stage[:, :, h * WIN:(h + 1) * WIN, :].reshape(n, D).astype(bf16) for h in range(PER * m, PER * (m + 1))], axis=0)
            dq_ref[m] = collapse(dot(e, w_ref[m, :, 64:256]), n).astype(bf16)
            gkv_ref[m, :, 0:192] = dot(e, expand(q_ref[m]), 0, 0).astype(bf16)

def back(rank, wlo, whi, encoded, a_full, qk, p, c, mx, lse_loc, lse, delta, dctx, q):
    micros, n = encoded.shape[0], mx.shape[0]
    pairs = n // micros
    tiles = wlo.shape[1]
    wins = pairs // WIN
    sd = jax.ShapeDtypeStruct
    def whole(x):
        return pl.BlockSpec(x.shape, lambda g, *_: (0,) * x.ndim)
    rest = (qk, p, c, mx, lse_loc, lse, delta, dctx, q)
    return pl.pallas_call(
        functools.partial(back_kernel, micros, pairs, tiles),
        out_shape=(sd((micros, tiles * TILE, D), bf16), sd((4, n, 192), bf16), sd((4, D, 384), bf16)),
        grid_spec=pltpu.PrefetchScalarGridSpec(
            num_scalar_prefetch=3, grid=(micros * tiles,),
            in_specs=[pl.BlockSpec((1, TILE, D), lambda g, r, lo, hi: (g // tiles, r[0] * tiles + g % tiles, 0)),
                      pl.BlockSpec(memory_space=pl.ANY)] + [whole(x) for x in rest],
            out_specs=[pl.BlockSpec((1, TILE, D), lambda g, r, lo, hi: (g // tiles, g % tiles, 0)),
                       pl.BlockSpec((4, n, 192), lambda g, *_: (0, 0, 0)), pl.BlockSpec((4, D, 384), lambda g, *_: (0, 0, 0))],
            scratch_shapes=[pltpu.VMEM((4, D, 512), bf16), pltpu.VMEM((micros, wins, 128, D), f32), pltpu.VMEM((micros, wins, 256, D), bf16),
                            pltpu.VMEM((micros, wins, 1, 128), f32), pltpu.VMEM((micros, wins, 1, 128), f32), pltpu.VMEM((TILE, D), f32),
                            pltpu.SemaphoreType.DMA]),
        compiler_params=pltpu.CompilerParams(vmem_limit_bytes=VMEM, dimension_semantics=("arbitrary",)),
        name="attention_backward",
    )(rank, wlo, whi, encoded, a_full, *rest)

def plan(seg_lengths, rank, tokens):
    micros, pairs = seg_lengths.shape
    ends = jnp.cumsum(seg_lengths, axis=1)
    starts = ends - seg_lengths
    span = tokens // 4
    tiles = span // TILE
    firsts = rank * span + TILE * jnp.arange(tiles, dtype=jnp.int32)
    def window(at):
        return jnp.sum((ends[:, None, :] <= at[None, :, None]).astype(jnp.int32), axis=-1) // WIN
    wlo, whi = window(firsts), window(firsts + (TILE - 1))
    def lanes(x):
        x = jnp.broadcast_to(x.reshape(micros, pairs // WIN, 1, 1, WIN), (micros, pairs // WIN, 1, HEADS, WIN))
        return jnp.pad(x.reshape(micros, pairs // WIN, 1, HEADS * WIN), ((0, 0), (0, 0), (0, 0), (0, 128 - HEADS * WIN)))
    return wlo, whi, lanes(starts), lanes(ends)

def put(src, dst, ssem, rsem, where):
    return pltpu.make_async_remote_copy(src_ref=src, dst_ref=dst, send_sem=ssem, recv_sem=rsem, device_id=where, device_id_type=MESH)

def flips(m):
    return (m + 2) % 4, m + 1 - 2 * (m % 2)

def gelu(u):
    c = math.sqrt(2.0 / math.pi)
    t = jnp.tanh(c * (u + 0.044715 * u * u * u))
    return 0.5 * u * (1.0 + t), 0.5 * (1.0 + t) + 0.5 * u * (1.0 - t * t) * c * (1.0 + 3 * 0.044715 * u * u)

def norm_back(y, r, pushed):
    return r * (pushed - y * jnp.mean(pushed * y, axis=-1, keepdims=True))

def merge(ca, la, cb, lb):
    top = jnp.maximum(la, lb)
    ea, eb = jnp.exp(la - top), jnp.exp(lb - top)
    total = ea + eb
    wa, wb = ea / total, eb / total
    n = la.shape[0]
    return [ca[m].astype(f32) * per_head(wa, m, n) + cb[m].astype(f32) * per_head(wb, m, n) for m in range(4)], top + jnp.log(total)

def middle_kernel(groups, weight, ctxl_ref, lsel_ref, x1_ref, a_hbm, b_hbm, dir_ref, keyc, slotc, keyr, slotr, rel_ref,
                  ctx_ref, lse_ref, dctx_ref, delta_ref, x3_ref, dx2_ref, y3_ref, du_ref, p3_ref, hs_ref,
                  co, ffi, ffo, cbuf, lbuf, cmid, lmid, msgs, hsum, xbuf, xmid, nbuf, nmid,
                  lsem, csem, crec, msem, mrec, hsem, hrec, xsem, xrec, nsem, nrec):
    n = x1_ref.shape[0]
    total = 4 * groups
    d, m = lax.axis_index("dp"), lax.axis_index("mp")
    me = d * 4 + m
    xm, cm = flips(m)
    loads = [pltpu.make_async_copy(a_hbm.at[:, :, 896:1152], co, lsem.at[0]),
             pltpu.make_async_copy(b_hbm.at[:, 0:768], ffi, lsem.at[1]),
             pltpu.make_async_copy(b_hbm.at[:, 768:1536], ffo, lsem.at[2])]
    for load in loads:
        load.start()
    barrier = pltpu.get_barrier_semaphore()
    def hello(j, _):
        to = (me + j) % total
        pl.semaphore_signal(barrier, inc=1, device_id=(to // 4, to % 4), device_id_type=MESH)
        return 0
    lax.fori_loop(1, total, hello, 0)
    pl.semaphore_wait(barrier, total - 1)
    hop = [put(ctxl_ref, cbuf.at[0], csem.at[0], crec.at[0], (d, cm)), put(lsel_ref, lbuf.at[0], csem.at[1], crec.at[1], (d, cm))]
    for c in hop:
        c.start()
    for c in hop:
        c.wait()
    both, lse = merge(ctxl_ref, lsel_ref[...], cbuf.at[0], lbuf[0])
    for k in range(4):
        cmid[k] = both[k].astype(bf16)
    lmid[...] = lse
    hop = [put(cmid, cbuf.at[1], csem.at[2], crec.at[2], (d, xm)), put(lmid, lbuf.at[1], csem.at[3], crec.at[3], (d, xm))]
    for c in hop:
        c.start()
    for load in loads:
        load.wait()
    direction = dir_ref[...]
    fd = dot(jnp.broadcast_to(direction, (8, D)).astype(bf16), ffo[...])[0:1]
    for c in hop:
        c.wait()
    both, lse = merge(cmid, lmid[...], cbuf.at[1], lbuf[1])
    lse_ref[...] = lse
    x2 = x1_ref[...]
    for k in range(4):
        low = both[k].astype(bf16)
        ctx_ref[k] = low
        x2 = x2 + dot(low, co[k, :, 64:256], 1, 1)
    y3, r3 = rms(x2)
    y3b = y3.astype(bf16)
    y3_ref[...] = y3b
    act, slope = gelu(dot(y3b, ffi[...]))
    hid = act.astype(bf16)
    hidf = hid.astype(f32)
    score = jnp.sum(hidf * fd, axis=1, keepdims=True) + jnp.where(m == 0, jnp.sum(x2 * direction, axis=1, keepdims=True), 0.0)
    eye = lax.broadcasted_iota(jnp.int32, (n, n), 0) == lax.broadcasted_iota(jnp.int32, (n, n), 1)
    row = jnp.sum(jnp.where(eye, score, 0.0), axis=0, keepdims=True)
    line = lax.broadcasted_iota(jnp.int32, (8, n), 0)
    msgs[me] = jnp.where(line == 0, row, jnp.where(line == 1, rel_ref[...], 0.0))
    def tell(j, _):
        to = (me + j) % total
        put(msgs.at[me], msgs.at[me], msem.at[j], mrec.at[me], (to // 4, to % 4)).start()
        return 0
    lax.fori_loop(1, total, tell, 0)
    x3p = dot(hid, ffo[...], 1, 1)
    xmid[0] = x3p.astype(bf16)
    xhop = put(xmid.at[0], xbuf.at[0], xsem.at[0], xrec.at[0], (d, cm))
    xhop.start()
    def hear(j, _):
        to = (me + j) % total
        put(msgs.at[to], msgs.at[to], msem.at[j], mrec.at[to], (to // 4, to % 4)).wait_recv()
        put(msgs.at[me], msgs.at[me], msem.at[j], mrec.at[me], (to // 4, to % 4)).wait_send()
        return 0
    lax.fori_loop(1, total, hear, 0)
    kc, sc = keyc[...], slotc[...]
    lane = lax.broadcasted_iota(jnp.int32, (1, n), 1)
    half = n // 2
    def rows_of(g):
        s = (msgs[4 * g] + msgs[4 * g + 1] + msgs[4 * g + 2] + msgs[4 * g + 3])[0:1]
        rel = msgs[4 * g][1:2]
        slot = (lane // half) * (groups * half) + g * half + lane % half
        return s, rel, keyr[pl.ds(g, 1), :] == kc, slotr[pl.ds(g, 1), :] == sc, slot // 16 == kc, slot == sc
    def tops(g, carry):
        a, b, own, rown = carry
        s, rel, same, mine, rsame, rmine = rows_of(g)
        return (jnp.maximum(a, jnp.where(same, s, FAR)), jnp.maximum(b, jnp.where(rsame, rel, FAR)),
                own + jnp.where(mine, s, 0.0), rown + jnp.where(rmine, rel, 0.0))
    z = jnp.zeros((n, n), f32)
    far = jnp.full((n, n), FAR, f32)
    a, b, own, rown = lax.fori_loop(0, groups, tops, (far, far, z, z), unroll=groups <= 8)
    a, b = jnp.max(a, axis=1, keepdims=True), jnp.max(b, axis=1, keepdims=True)
    own, rown = jnp.sum(own, axis=1, keepdims=True), jnp.sum(rown, axis=1, keepdims=True)
    def sums(g, carry):
        s, rel, same, _, rsame, _ = rows_of(g)
        return (carry[0] + jnp.where(same, jnp.exp(s - a), 0.0), carry[1] + jnp.where(rsame, jnp.exp(rel - b), 0.0))
    sa, sb = lax.fori_loop(0, groups, sums, (z, z), unroll=groups <= 8)
    dscore = weight * (jnp.exp(own - a) / jnp.sum(sa, axis=1, keepdims=True) - jnp.exp(rown - b) / jnp.sum(sb, axis=1, keepdims=True))
    du = (slope * dscore * fd).astype(bf16)
    du_ref[...] = du
    nmid[0] = dot(du, ffi[...], 1, 1).astype(bf16)
    nhop = put(nmid.at[0], nbuf.at[0], nsem.at[0], nrec.at[0], (d, cm))
    nhop.start()
    hsum[d] = jnp.broadcast_to(jnp.sum(hidf * dscore, axis=0, keepdims=True), (8, D))
    def spread(j, _):
        to = (d + j) % groups
        put(hsum.at[d], hsum.at[d], hsem.at[j], hrec.at[d], (to, m)).start()
        return 0
    lax.fori_loop(1, groups, spread, 0)
    nhop.wait()
    part = nmid[0].astype(f32) + nbuf[0].astype(f32)
    nmid[1] = part.astype(bf16)
    nhop = put(nmid.at[1], nbuf.at[1], nsem.at[1], nrec.at[1], (d, xm))
    nhop.start()
    xhop.wait()
    xpart = x3p + xbuf[0].astype(f32)
    xmid[1] = xpart.astype(bf16)
    xhop = put(xmid.at[1], xbuf.at[1], xsem.at[1], xrec.at[1], (d, xm))
    xhop.start()
    nhop.wait()
    dn3 = part + nbuf[1].astype(f32)
    p3_ref[...] = (dn3 * y3).astype(bf16)
    dx2 = dscore * direction + norm_back(y3, r3, dn3)
    dx2_ref[...] = dx2
    gc = dx2.astype(bf16)
    delta = jnp.zeros((n, 128), f32)
    for k in range(4):
        dctx = dot(gc, co[k, :, 64:256]).astype(bf16)
        dctx_ref[k] = dctx
        pick = (lax.broadcasted_iota(jnp.int32, (192, 128), 0) // HEAD + PER * k == lax.broadcasted_iota(jnp.int32, (192, 128), 1)).astype(f32)
        delta = delta + exact(dctx.astype(f32) * both[k], pick)
    delta_ref[...] = delta
    xhop.wait()
    x3_ref[...] = x2 + xpart + xbuf[1].astype(f32)
    def gathered(j, acc):
        to = (d + j) % groups
        put(hsum.at[to], hsum.at[to], hsem.at[j], hrec.at[to], (to, m)).wait_recv()
        put(hsum.at[d], hsum.at[d], hsem.at[j], hrec.at[d], (to, m)).wait_send()
        return acc + hsum[to]
    hs_ref[...] = lax.fori_loop(1, groups, gathered, hsum[d])

def middle(groups, weight, ctxl, lsel, x1, a_full, b_full, direction, keyc, slotc, keyr, slotr, rel):
    n = x1.shape[0]
    sd = jax.ShapeDtypeStruct
    any_, vm = (pl.BlockSpec(memory_space=s) for s in (pl.ANY, pltpu.VMEM))
    S, V = pltpu.SemaphoreType.DMA, pltpu.VMEM
    return pl.pallas_call(
        functools.partial(middle_kernel, groups, weight),
        out_shape=(sd((4, n, 192), bf16), sd((n, 128), f32), sd((4, n, 192), bf16), sd((n, 128), f32), sd((n, D), f32), sd((n, D), f32),
                   sd((n, D), bf16), sd((n, D), bf16), sd((n, D), bf16), sd((8, D), f32)),
        in_specs=[vm, vm, vm, any_, any_] + [vm] * 6, out_specs=[vm] * 10,
        scratch_shapes=[V((4, D, 256), bf16), V((D, D), bf16), V((D, D), bf16), V((2, 4, n, 192), bf16), V((2, n, 128), f32), V((4, n, 192), bf16), V((n, 128), f32),
                        V((4 * groups, 8, n), f32), V((groups, 8, D), f32), V((2, n, D), bf16), V((2, n, D), bf16), V((2, n, D), bf16), V((2, n, D), bf16),
                        S((3,)), S((4,)), S((4,)), S((4 * groups,)), S((4 * groups,)), S((groups,)), S((groups,)), S((2,)), S((2,)), S((2,)), S((2,))],
        compiler_params=pltpu.CompilerParams(collective_id=1, has_side_effects=True, vmem_limit_bytes=VMEM),
        name="feed_forward",
    )(ctxl, lsel, x1, a_full, b_full, direction, keyc, slotc, keyr, slotr, rel)

def tail_kernel(groups, dqp_ref, gkv_ref, x0_ref, x1_ref, dx2_ref, v1_ref, ctx_ref, y3_ref, du_ref, p3_ref, a_hbm,
                dx0_ref, out0, out1,
                w, dqm, dqb, dqs, dvs, kvb, kvx, kvs, r0, r1, yb0, yb1, ys0, ys1, zl0, zl1, zr0, zr1,
                wsem, qsem, qrec, ksem, krec, ysem, yrec, zsem, zrec):
    n = x0_ref.shape[0]
    lines = groups // 2
    rows = D // groups
    d, m = lax.axis_index("dp"), lax.axis_index("mp")
    o, i = d // 2, d % 2
    dy = d + 1 - 2 * i
    xm, cm = flips(m)
    xcm = (cm + 2) % 4
    load = pltpu.make_async_copy(a_hbm.at[:, :, 0:640], w, wsem)
    load.start()
    barrier = pltpu.get_barrier_semaphore()
    def hello(dd, mm):
        pl.semaphore_signal(barrier, inc=1, device_id=(dd, mm), device_id_type=MESH)
    hello(dy, m); hello(d, xm); hello(d, cm)
    pl.when(o + 1 < lines)(lambda: hello(d + 2, m))
    pl.when(o > 0)(lambda: hello(d - 2, m))
    pl.semaphore_wait(barrier, 3 + jnp.where(o + 1 < lines, 1, 0) + jnp.where(o > 0, 1, 0))
    qhop = put(dqp_ref, dqb.at[0], qsem.at[0], qrec.at[0], (d, cm))
    qhop.start()
    khops = [put(gkv_ref.at[cm], kvb.at[0], ksem.at[0], krec.at[0], (d, cm)), put(gkv_ref.at[xcm], kvb.at[1], ksem.at[1], krec.at[1], (d, cm))]
    for c in khops:
        c.start()
    def keep(ref, value):
        for g in range(groups):
            ref[g] = value[g * rows:(g + 1) * rows].astype(bf16)
    ones = jnp.ones((n, 64), bf16)
    lane = lax.broadcasted_iota(jnp.int32, (n, 64), 1)
    y3 = y3_ref[...]
    gc = dx2_ref[...].astype(bf16)
    keep(r0, jnp.concatenate([dot(y3, du_ref[...], 0, 0), dot(gc, ctx_ref[m], 0, 0), dot(p3_ref[...], ones, 0, 0)], axis=1))
    def across(k, r, yb):
        return [put(r.at[2 * oo + 1 - i], yb.at[oo], ysem.at[k, oo], yrec.at[k, oo], (dy, m)) for oo in range(lines)]
    y0 = across(0, r0, yb0)
    for c in y0:
        c.start()
    qhop.wait()
    for k in range(4):
        dqm[k] = (dqp_ref[k].astype(f32) + dqb[0, k].astype(f32)).astype(bf16)
    qhop = put(dqm, dqb.at[1], qsem.at[1], qrec.at[1], (d, xm))
    qhop.start()
    for c in khops:
        c.wait()
    kvs[...] = (gkv_ref[xm].astype(f32) + kvb[1].astype(f32)).astype(bf16)
    khop = put(kvs, kvx, ksem.at[2], krec.at[2], (d, xm))
    khop.start()
    load.wait()
    x1 = x1_ref[...]
    y1, g1 = rms(x0_ref[...].astype(f32))
    y2, g2 = rms(x1)
    qhop.wait()
    dn2 = 0
    for k in range(4):
        dq = (dqm[k].astype(f32) + dqb[1, k].astype(f32)).astype(bf16)
        dqs[k] = dq
        dn2 = dn2 + dot(dq, w[k, :, WQ:WQ + 192], 1, 1)
    dx1 = dx2_ref[...] + norm_back(y2, g2, dn2)
    gs = dx1.astype(bf16)
    dn1 = 0
    for k in range(4):
        dv = dot(gs, w[k, :, SO:SO + 192]).astype(bf16)
        dvs[k] = dv
        dn1 = dn1 + dot(dv, w[k, :, SV:SV + 192], 1, 1)
    dx0_ref[...] = dx1 + norm_back(y1, g1, dn1)
    small = [dot(y1.astype(bf16), dvs[m], 0, 0), dot(gs, v1_ref[m], 0, 0), dot(y2.astype(bf16), dqs[m], 0, 0)]
    gains = (dot((dn1 * y1).astype(bf16), jnp.where(lane < 32, ones, 0), 0, 0) + dot((dn2 * y2).astype(bf16), jnp.where(lane < 32, 0, ones), 0, 0))
    khop.wait()
    kv = gkv_ref[m].astype(f32) + kvb[0].astype(f32) + kvx[...].astype(f32)
    keep(r1, jnp.concatenate(small + [kv, gains], axis=1))
    y1c = across(1, r1, yb1)
    for c in y1c:
        c.start()
    def line(k, copies, r, yb, ys, zl, zr):
        for oo in range(lines):
            copies[oo].wait()
            ys[oo] = (r[2 * oo + i].astype(f32) + yb[oo].astype(f32)).astype(bf16)
        def right(t):
            return put(ys.at[t], zl.at[t], zsem.at[k, t], zrec.at[k, 0, t], (d + 2, m))
        def left(t):
            return put(ys.at[t], zr.at[t], zsem.at[k, t], zrec.at[k, 1, t], (d - 2, m))
        def from_left(t):
            put(ys.at[t], zl.at[t], zsem.at[k, t], zrec.at[k, 0, t], (d - 2, m)).wait_recv()
        def from_right(t):
            put(ys.at[t], zr.at[t], zsem.at[k, t], zrec.at[k, 1, t], (d + 2, m)).wait_recv()
        def add(t, z):
            ys[t] = (ys[t].astype(f32) + z[t].astype(f32)).astype(bf16)
        for j in range(lines - 1):
            t = lines - 1 - j
            def go_right(t=t):
                @pl.when(o > 0)
                def _():
                    from_left(t)
                    add(t, zl)
                right(t).start()
            pl.when(o < t)(go_right)
            s = j
            def go_left(s=s):
                @pl.when(o < lines - 1)
                def _():
                    from_right(s)
                    add(s, zr)
                left(s).start()
            pl.when(o > s)(go_left)
        def finish(out):
            out[...] = ys[o].astype(f32)
            @pl.when(o > 0)
            def _():
                from_left(o)
                out[...] = out[...] + zl[o].astype(f32)
            @pl.when(o < lines - 1)
            def _():
                from_right(o)
                out[...] = out[...] + zr[o].astype(f32)
            for t in range(lines):
                pl.when(o < t)(lambda t=t: right(t).wait_send())
                pl.when(o > t)(lambda t=t: left(t).wait_send())
        return finish
    f0 = line(0, y0, r0, yb0, ys0, zl0, zr0)
    f1 = line(1, y1c, r1, yb1, ys1, zl1, zr1)
    f0(out0)
    f1(out1)

def tail(groups, dqp, gkv, x0, x1, dx2, v1, ctx, y3, du, p3, a_full):
    n = x0.shape[0]
    rows, lines = D // groups, groups // 2
    sd = jax.ShapeDtypeStruct
    any_, vm = (pl.BlockSpec(memory_space=s) for s in (pl.ANY, pltpu.VMEM))
    S, V = pltpu.SemaphoreType.DMA, pltpu.VMEM
    blocks = lambda k: V((k, rows, 1024), bf16)
    return pl.pallas_call(
        functools.partial(tail_kernel, groups),
        out_shape=(sd((n, D), f32), sd((rows, 1024), f32), sd((rows, 1024), f32)),
        in_specs=[vm] * 10 + [any_], out_specs=[vm] * 3,
        scratch_shapes=[V((4, D, 640), bf16), V((4, n, 192), bf16), V((2, 4, n, 192), bf16), V((4, n, 192), bf16), V((4, n, 192), bf16),
                        V((2, D, 384), bf16), V((D, 384), bf16), V((D, 384), bf16), blocks(groups), blocks(groups)] + [blocks(lines)] * 8 +
                       [S, S((2,)), S((2,)), S((3,)), S((3,)), S((2, lines)), S((2, lines)), S((2, lines)), S((2, 2, lines))],
        compiler_params=pltpu.CompilerParams(collective_id=2, has_side_effects=True, vmem_limit_bytes=VMEM),
        name="gradient_sums",
    )(dqp, gkv, x0, x1, dx2, v1, ctx, y3, du, p3, a_full)

def shards(dec_in, encoded, seg_lengths, pair_slot, relevance, score_dir, gain_self, gain_cross, gain_ff,
           self_value, self_out, cross_query, cross_key, cross_value, cross_out, ff_in, ff_out):
    micros, pairs = dec_in.shape[0], dec_in.shape[1]
    n = micros * pairs
    groups = lax.axis_size("dp")
    d, m = lax.axis_index("dp"), lax.axis_index("mp")
    gains = [g.astype(f32)[:, None] for g in (gain_self, gain_cross, gain_ff)]
    def scaled(g, weight):
        return (g * weight.astype(f32)).astype(bf16)
    a_own = jnp.concatenate([scaled(gains[0], self_value), self_out.T, scaled(gains[1], cross_query), cross_key, cross_value, cross_out.T], axis=1)
    b_own = jnp.concatenate([scaled(gains[2], ff_in), ff_out.T], axis=1)
    a_full, b_full = gather(groups, a_own, b_own)
    a_full, b_full = a_full.reshape(4, D, 1152), b_full.reshape(D, 1536)
    rank = jnp.reshape(m, (1,)).astype(jnp.int32)
    wlo, whi, lo, hi = plan(seg_lengths[:, 0], m, encoded.shape[1])
    x0 = dec_in.reshape(n, D)
    x1, v1, q, qk, p, c, mx, ctxl, lsel = front(rank, wlo, whi, x0, a_full, encoded, lo, hi)
    everyone = groups * pairs
    slots = pair_slot + everyone * jnp.arange(micros, dtype=jnp.int32)[:, None]
    slotr = slots.reshape(micros, groups, pairs).transpose(1, 0, 2).reshape(groups, n)
    slotc = lax.dynamic_slice_in_dim(slotr, d, 1, 0).reshape(n, 1)
    direction = score_dir.astype(f32)
    ctx, lse, dctx, delta, x3, dx2, y3, du, p3, hs = middle(
        groups, CAND * math.sqrt(D), ctxl, lsel, x1, a_full, b_full, direction.reshape(1, D),
        slotc // CAND, slotc, slotr // CAND, slotr, relevance.reshape(1, n))
    d_encoded, dqp, gkv = back(rank, wlo, whi, encoded, a_full, qk, p, c, mx, lsel, lse, delta, dctx, q)
    dx0, sum0, sum1 = tail(groups, dqp, gkv, x0, x1, dx2, v1, ctx, y3, du, p3, a_full)
    here = lax.dynamic_slice_in_dim(direction, d * (D // groups), D // groups)
    return (
        x3.reshape(micros, pairs, D),
        dx0.reshape(micros, pairs, D),
        d_encoded,
        sum1[:, 960] / gains[0][:, 0],
        sum1[:, 992] / gains[1][:, 0],
        sum0[:, 960] / gains[2][:, 0],
        sum1[:, 0:192] * gains[0],
        sum1[:, 192:384].T,
        sum1[:, 384:576] * gains[1],
        sum1[:, 576:768],
        sum1[:, 768:960],
        sum0[:, 768:960].T,
        sum0[:, 0:768] * gains[2],
        hs[0][:, None] * here[None, :],
    )


def solution(mesh):
    in_specs = (
        P(None, "dp", None),
        P(None, "dp", None),
        P(None, "dp", None),
        P(),
        P(None, "dp"),
        P(),
        P("dp"),
        P("dp"),
        P("dp"),
        P("dp", "mp"),
        P("mp", "dp"),
        P("dp", "mp"),
        P("dp", "mp"),
        P("dp", "mp"),
        P("mp", "dp"),
        P("dp", "mp"),
        P("mp", "dp"),
    )
    out_specs = (
        P(None, "dp", None),
        P(None, "dp", None),
        P(None, ("dp", "mp"), None),
        P("dp"),
        P("dp"),
        P("dp"),
        P("dp", "mp"),
        P("mp", "dp"),
        P("dp", "mp"),
        P("dp", "mp"),
        P("dp", "mp"),
        P("mp", "dp"),
        P("dp", "mp"),
        P("mp", "dp"),
    )
    return jax.shard_map(shards, mesh=mesh, in_specs=in_specs, out_specs=out_specs, check_vma=False)
```

time: 1230 us -> 275 us (0.22)
  waiting for transfers between devices: 493 us -> 0 us
  blocking collectives: 250 us -> 0 us
  Pallas kernels: 0 us -> 241 us
  matrix products: 216 us -> 0 us
  other arithmetic: 129 us -> 17 us
  local copies, waits for them, and re-layouts: 70.2 us -> 14 us
  starting transfers between devices: 41.9 us -> 0 us
  between operations: 18.6 us -> 0.86 us
    pallas_call x0 -> x5, Pallas kernels: none -> 241 us  [the longest x1 68.4 us: gather(): pl.pallas_call(functools.partial(gather_kernel, groups, ra), out_shape=ou...]
    dot_general x52 -> x0, matrix products: 216 us -> none  [product(): return jnp.einsum(form, left, right, preferred_element_type=jnp.float32)]
    reduce_scatter x4 -> x0, waiting for transfers between devices: 210 us -> none  [the longest x1 72.2 us: shards(): lax.psum_scatter(local_grads[10], 'dp', scatter_dimension=1, tiled=True)]
    all_gather x6 -> x0, blocking collectives: 190 us -> none  [the longest x1 33.1 us: fetch(): lax.all_gather(cross_value, 'dp', axis=0, tiled=True)]
    all_to_all x8 -> x0, waiting for transfers between devices: 114 us -> none  [the longest x2 64 us: shards(): lax.all_to_all(grad_key, 'mp', split_axis=0, concat_axis=1, tiled=True)]
    psum x6 -> x0, waiting for transfers between devices: 92.9 us -> none  [head_total(): return lax.psum(partial_value, 'mp')]
    unnamed x2 -> x0, blocking collectives: 59.8 us -> none
    all_gather x4 -> x0, waiting for transfers between devices: 47.6 us -> none  [the longest x1 40.5 us: fetch(): lax.all_gather(ff_out, 'dp', axis=1, tiled=True)]
  transfers between devices with their start and end apart: 26 -> 0, of which waited for: 15 -> 0; matrix products, arithmetic and copies ran while one was open for 18% -> 0% of each run, Pallas kernels for 0% -> 0%
where the time goes in v1:
time: 275 us; the launch traced here: 273 us
  Pallas kernels  241 us (88%)
  other arithmetic  17 us (6%)
  local copies, waits for them, and re-layouts  14 us (5%)
    pallas_call x1, Pallas kernels, gather(): pl.pallas_call(functools.partial(gather_kernel, groups, ra), out_shape=ou...  68.4 us
    pallas_call x1, Pallas kernels, tail(): pl.pallas_call(functools.partial(tail_kernel, groups), out_shape=(sd((n,...  67.4 us
    pallas_call x1, Pallas kernels, back(): pl.pallas_call(functools.partial(back_kernel, micros, pairs, tiles), out_...  38.4 us
    pallas_call x1, Pallas kernels, middle(): pl.pallas_call(functools.partial(middle_kernel, groups, weight), out_shap...  37.8 us
    pallas_call x1, Pallas kernels, front(): pl.pallas_call(functools.partial(front_kernel, micros, pairs, tiles), out...  29 us

profile of v1, /device:TPU:0, one launch (start us, length us, event | category | flops | bytes accessed | tf_op | source)
XLA Modules:
  0.0 272.9 jit_solution(14988794457060278663)
XLA Ops:
  0.6 0.7 convert_element_type.38
  1.3 0.7 convert_element_type.41
  2.0 0.9 multiply_convert_fusion.1
  2.9 0.9 copy.61
  3.8 0.9 copy.62
  4.7 1.7 concatenate.6.a_ref
  6.3 0.7 convert_element_type.44
  7.0 1.0 multiply_convert_fusion
  8.0 1.6 pad_maximum_fusion.b_ref
  9.6 68.4 %gather_weights.1 = (bf16[4,8,96,1152]{3,2,1,0:T(8,128)(2,1)}, bf16[8,96,1536]{2,1,0:T(8,128)(2,1)}) custom-call(bf16[96,1152]{1,0:T(8,128)(2,1)} %concatenate.6.a_ref, bf16[96,1536]{1,0:T(8,128)(2,1)} %pad_maximum_fusion.b_ref), custom_call_target="tpu_custom_call" | custom-call | tf_op jit(solution)/shard_map/gather_weights/pallas_call | solution.py:121
  78.1 0.9 reduce_window_sum.13
  79.6 0.6 and_select_fusion.whi
  81.5 1.3 reduce.11
  83.1 0.6 pad.7.lo_ref
  83.8 0.6 pad.8.hi_ref
  84.4 29.0 %attention_forward.1 = (f32[128,768]{1,0:T(8,128)}, bf16[4,128,192]{2,1,0:T(8,128)(2,1)}, bf16[4,128,192]{2,1,0:T(8,128)(2,1)}, bf16[2,8,128,768]{3,2,1,0:T(8,12...) custom-call(s32[1]{0:T(128)} %bitcast.rank_ref, ...), custom_call_target="tpu_custom_call" | custom-call | tf_op jit(solution)/shard_map/attention_forward/pallas_call | solution.py:275
  113.8 0.7 add_select_fusion.keyc
  114.4 0.6 add_select_fusion.1.keyr
  116.2 37.8 %feed_forward.1 = (bf16[4,128,192]{2,1,0:T(8,128)(2,1)}, f32[128,128]{1,0:T(8,128)}, bf16[4,128,192]{2,1,0:T(8,128)(2,1)}, f32[128,128]{1,0:T(8,128)}, f32[128,7...) custom-call(bf16[4,128,192]{2,1,0:T(8,128)(2,1)} %get-tuple-element., ...), custom_call_target="tpu_custom_call" | custom-call | tf_op jit(solution)/shard_map/feed_forward/pallas_call | solution.py:540
  154.0 38.4 %attention_backward.1 = (bf16[2,3072,768]{2,1,0:T(8,128)(2,1)}, bf16[4,128,192]{2,1,0:T(8,128)(2,1)}, bf16[4,768,384]{2,1,0:T(8,128)(2,1)}) custom-call(s32[1]{0:T(128)} %bitcast.rank_ref, s32[2,12]{1,0:T(2,128)} %and_select_fusion.1.wlo, s32[2,12]{1,0:T(2,128)} %and_select_fusion.whi, bf16[2,12288,768]{2,1,0:T(8,128)(2,1)} %enc_ref.1, ...), custom_call_target="tpu_custom_call" | custom-call | tf_op jit(solution)/shard_map/attention_backward/pallas_call | solution.py:344
  192.5 67.4 %gradient_sums.1 = (f32[128,768]{1,0:T(8,128)}, f32[96,1024]{1,0:T(8,128)}, f32[96,1024]{1,0:T(8,128)}) custom-call(bf16[4,128,192]{2,1,0:T(8,128)(2,1)} %get-tuple-element.55.dqp_ref, bf16[4,768,384]{2,1,0:T(8,128)(2,1)} %get-tuple-element.56.gkv_ref, bf16[128,768]{1,0:T(8,128)(2,1)} %bitcast.27, f32[128,768]{1,0:T(8,128)} %get-tuple-element.44.x1_ref, ...), custom_call_target="tpu_custom_call" | custom-call | tf_op jit(solution)/shard_map/gradient_sums/pallas_call | solution.py:684
  259.9 2.0 fusion.6
  261.9 0.7 copy.71
  262.7 1.8 slice_multiply_fusion
  264.4 0.9 slice_bitcast_fusion
  265.3 0.7 copy.72
  266.1 1.1 slice_reduce_fusion.1
  268.2 1.0 slice_reduce_fusion
  269.7 0.8 slice_reduce_fusion.3
  270.6 0.8 broadcast_multiply_fusion
  271.4 0.7 copy.77
  272.1 0.7 copy.78
  (46 shorter events, 5.5 us)
Async XLA Ops:
  84.4 29.0 %copy-start.4 = (s32[2,512]{1,0:T(2,128)S(1)}, s32[2,512]{1,0:T(2,128)}, u32[]{:S(2)}) copy-start(s32[2,512]{1,0:T(2,128)} %param.20) | copy-start | bytes 12292
  84.4 30.7 %copy-start.5 = (bf16[768]{0:T(1024)(128)(2,1)S(1)}, bf16[768]{0:T(1024)(128)(2,1)}, u32[]{:S(2)}) copy-start(bf16[768]{0:T(1024)(128)(2,1)} %param.22) | copy-start | bytes 4612
  84.4 31.2 %copy-start.6 = (f32[2,64]{1,0:T(2,128)S(1)}, f32[2,64]{1,0:T(2,128)}, u32[]{:S(2)}) copy-start(f32[2,64]{1,0:T(2,128)} %param.21) | copy-start | bytes 1540
  113.6 2.6 copy-start.3
  113.8 2.5 copy-start
  192.4 74.7 %copy-start.7 = (bf16[96]{0:T(256)(128)(2,1)S(1)}, bf16[96]{0:T(256)(128)(2,1)}, u32[]{:S(2)}) copy-start(bf16[96]{0:T(256)(128)(2,1)} %param.24) | copy-start | bytes 580
  192.5 75.2 %copy-start.8 = (bf16[96]{0:T(256)(128)(2,1)S(1)}, bf16[96]{0:T(256)(128)(2,1)}, u32[]{:S(2)}) copy-start(bf16[96]{0:T(256)(128)(2,1)} %param.23) | copy-start | bytes 580
  192.5 76.7 %copy-start.9 = (bf16[96]{0:T(256)(128)(2,1)S(1)}, bf16[96]{0:T(256)(128)(2,1)}, u32[]{:S(2)}) copy-start(bf16[96]{0:T(256)(128)(2,1)} %param.25) | copy-start | bytes 580
  192.5 78.9 %copy-start.1 = (f32[128,768]{1,0:T(8,128)S(1)}, f32[128,768]{1,0:T(8,128)}, u32[]{:S(2)}) copy-start(f32[128,768]{1,0:T(8,128)} %get-tuple-element.46) | copy-start | bytes 1179652
  259.9 12.2 %copy-start.2 = (f32[128,768]{1,0:T(8,128)S(1)}, f32[128,768]{1,0:T(8,128)}, u32[]{:S(2)}) copy-start(f32[128,768]{1,0:T(8,128)} %get-tuple-element.63) | copy-start | bytes 1179652

commit v2 on v0

v2 whole, which is shorter than its diff:
```python
import functools
import math

import jax
import jax.numpy as jnp
from jax import lax
from jax.experimental import pallas as pl
from jax.experimental.pallas import tpu as pltpu
from jax.sharding import PartitionSpec as P

MESH = pl.DeviceIdType.MESH
bf16, f32 = jnp.bfloat16, jnp.float32
CAND = 16
D, HEAD, HEADS = 768, 64, 12
PER = HEADS // 4
WIDE = PER * HEAD
WIN = 8
COLS = HEADS * WIN
TILE = 256
eps = 1e-6
FAR = -1e30
VMEM = 63 << 20
UNROLL = 2
OUTS = 2


def dot(a, b, ca=1, cb=0):
    return lax.dot_general(a, b, (((ca,), (cb,)), ((), ())), preferred_element_type=f32)


def exact(a, b):
    return lax.dot_general(a, b, (((1,), (0,)), ((), ())), preferred_element_type=f32, precision=lax.Precision.HIGHEST)


def iota(shape, axis):
    return lax.broadcasted_iota(jnp.int32, shape, axis)


def to_column(row):
    k = row.shape[1]
    return jnp.sum(jnp.where(iota((k, k), 0) == iota((k, k), 1), row, 0.0), axis=1, keepdims=True)


def to_row(column):
    k = column.shape[0]
    return jnp.sum(jnp.where(iota((k, k), 0) == iota((k, k), 1), column, 0.0), axis=0, keepdims=True)


def fold_row(row):
    parts = [row[:, k * 128:(k + 1) * 128] for k in range(D // 128)]
    return jnp.concatenate(parts + [jnp.zeros((8 - D // 128, 128), f32)], axis=0)


def unfold_row(x):
    return jnp.concatenate([x[k:k + 1] for k in range(D // 128)], axis=1)


def rms(v):
    r = lax.rsqrt(jnp.mean(v * v, axis=-1, keepdims=True) + eps)
    return v * r, r


def norm_back(y, r, pushed):
    return r * (pushed - y * jnp.mean(pushed * y, axis=-1, keepdims=True))


def gelu(u):
    c = math.sqrt(2.0 / math.pi)
    t = jnp.tanh(c * (u + 0.044715 * u * u * u))
    return 0.5 * u * (1.0 + t), 0.5 * (1.0 + t) + 0.5 * u * (1.0 - t * t) * c * (1.0 + 3 * 0.044715 * u * u)


def expand(x):
    col = iota(x.shape, 1) // HEAD
    return jnp.concatenate([jnp.where(col == j, x, 0) for j in range(PER)], axis=0)


def collapse(x, rows):
    out = 0
    for j in range(PER):
        part = x[j * rows:(j + 1) * rows]
        out = out + jnp.where(iota(part.shape, 1) // HEAD == j, part, 0)
    return out


def per_head(x, m, rows):
    col = iota((rows, WIDE), 1) // HEAD
    out = jnp.where(col == 0, x[:, PER * m:PER * m + 1], 0)
    for j in range(1, PER):
        out = jnp.where(col == j, x[:, PER * m + j:PER * m + j + 1], out)
    return out


def to_pairs(x):
    n = x.shape[0]
    wide = jnp.broadcast_to(x[:, None, :], (n, WIN, 128)).reshape(n * WIN, 128)
    wide = jnp.where(iota(wide.shape, 1) % WIN == iota(wide.shape, 0) % WIN, wide, 0.0)
    return exact(wide, (iota((128, 128), 0) // WIN == iota((128, 128), 1)).astype(f32))


def to_windows(x):
    wide = exact(x, (iota((128, 128), 0) == iota((128, 128), 1) // WIN).astype(f32))
    wide = jnp.where(iota(wide.shape, 1) % WIN == iota(wide.shape, 0) % WIN, wide, 0.0)
    return jnp.sum(wide.reshape(-1, WIN, 128), axis=1)


def put(src, dst, ssem, rsem, where):
    return pltpu.make_async_remote_copy(src_ref=src, dst_ref=dst, send_sem=ssem, recv_sem=rsem, device_id=where, device_id_type=MESH)


def flips(m):
    return (m + 2) % 4, m + 1 - 2 * (m % 2)


def merge(ca, la, cb, lb):
    top = jnp.maximum(la, lb)
    ea, eb = jnp.exp(la - top), jnp.exp(lb - top)
    total = ea + eb
    wa, wb = ea / total, eb / total
    n = la.shape[0]
    return [ca[m].astype(f32) * per_head(wa, m, n) + cb[m].astype(f32) * per_head(wb, m, n) for m in range(4)], top + jnp.log(total)


def blocks(ref):
    return [ref[m // 2, :, WIDE * (m % 2):WIDE * (m % 2 + 1)] for m in range(4)]


def fill(ref, values):
    for m in range(4):
        ref[m // 2, :, WIDE * (m % 2):WIDE * (m % 2 + 1)] = values[m].astype(ref.dtype)


def loop(first, end, body):
    whole = (end - first) // UNROLL

    def some(j, _):
        for i in range(UNROLL):
            body(first + j * UNROLL + i)
        return 0

    lax.fori_loop(0, whole, some, 0)
    for k in range(first + whole * UNROLL, end):
        body(k)


class Spread:
    def __init__(self, dst, sems, wide=False, early=False):
        self.dst, self.wide, self.early = dst, wide, early
        self.groups = dst.shape[1] if wide else dst.shape[0]
        self.lines = self.groups // 2
        self.snd, self.rz, self.ry, self.rx, self.rc, self.rq = (tuple(sems) + (None,) * 4)[:6]
        self.d, self.m = lax.axis_index("dp"), lax.axis_index("mp")
        self.o, self.i = self.d // 2, self.d % 2
        self.dy = self.d + 1 - 2 * self.i
        self.xm, self.cm = flips(self.m)

    def near(self, k):
        return (self.o + self.lines - k) % self.lines * 2 + self.i

    def far(self, k):
        return (self.o + self.lines - k) % self.lines * 2 + 1 - self.i

    def at(self, mm, dd):
        return self.dst.at[mm, dd] if self.wide else self.dst.at[dd]

    def send(self, mm, dd, way, sem, where):
        put(self.at(mm, dd), self.at(mm, dd), self.snd.at[way], sem, where).start()

    def got(self, mm, dd, sem):
        put(self.at(mm, dd), self.at(mm, dd), self.snd.at[0], sem, (self.d, self.xm)).wait_recv()

    def over(self, mm, k, sems):
        self.send(mm, self.near(k), 1, sems.at[k], (self.dy, self.m))

    def mates(self, dd, j):
        if self.wide:
            if j is not None:
                self.send(self.m, dd, 2, self.rx.at[j], (self.d, self.xm))
            self.send(self.m, dd, 3, self.rc.at[0], (self.d, self.cm))

    def own(self):
        for k in range(1, self.lines):
            self.send(self.m, self.d, 0, self.rz.at[k], ((self.o + k) % self.lines * 2 + self.i, self.m))
        self.over(self.m, 0, self.ry)
        self.mates(self.d, 0)

    def arrive(self, k):
        dd = self.near(k)
        self.got(self.m, dd, self.rz.at[k])
        if self.early:
            self.mates(dd, k)
            self.over(self.m, k, self.ry)
        else:
            self.over(self.m, k, self.ry)
            self.mates(dd, k)

    def across(self, k):
        dd = self.far(k)
        self.got(self.m, dd, self.ry.at[k])
        self.mates(dd, None if self.early else self.lines + k)

    def relay(self, j):
        dd = self.near(j) if j < self.lines else self.far(j - self.lines)
        self.got(self.xm, dd, self.rx.at[j])
        self.send(self.xm, dd, 4, self.rc.at[1], (self.d, self.cm))
        if self.early:
            self.over(self.xm, j, self.rq)

    def around(self, k):
        dd = self.far(k)
        self.got(self.xm, dd, self.rq.at[k])
        self.send(self.xm, dd, 4, self.rc.at[1], (self.d, self.cm))

    def events(self, start, pace):
        n, do = self.lines, functools.partial
        out = [(start + pace * k, do(self.arrive, k)) for k in range(1, n)]
        out += [(start + pace * (k + 1) + 1, do(self.across, k)) for k in range(n)]
        if self.early:
            out += [(start + 2 * pace * k + 3, do(self.relay, k)) for k in range(n)]
            out += [(start + 2 * pace * (k + 1) + 5, do(self.around, k)) for k in range(n)]
        elif self.wide:
            out += [(start + 2 * pace * j + 3, do(self.relay, j)) for j in range(2 * n)]
        return out

    def close(self):
        xcm = (self.cm + 2) % 4
        for sem, mm in ((0, self.cm), (1, xcm)):
            put(self.dst.at[mm], self.dst.at[mm], self.snd.at[0], self.rc.at[sem], (self.d, self.cm)).wait_recv()

    def sent(self):
        def done(way, pieces):
            ref = self.dst.at[0, pl.ds(0, pieces)] if self.wide else self.dst.at[pl.ds(0, pieces)]
            put(ref, ref, self.snd.at[way], self.rz.at[0], (self.d, self.cm)).wait_send()
        done(0, self.lines - 1)
        done(1, self.groups if self.early else self.lines)
        if self.wide:
            done(2, self.lines if self.early else self.groups)
            done(3, self.groups)
            done(4, self.groups)


class Reduce:
    def __init__(self, r, yb, ys, z, sems):
        self.lines, self.r, self.yb, self.ys, self.z = r.shape[0] // 2, r, yb, ys, z
        self.snd, self.yrec, self.zrec = sems
        self.d, self.m = lax.axis_index("dp"), lax.axis_index("mp")
        self.o, self.i = self.d // 2, self.d % 2
        self.order = list(range(1, self.lines)) + [0]

    def fill(self, value):
        groups, rows = self.r.shape[0], self.r.shape[1]
        for g in range(groups):
            self.r[g] = value[g * rows:(g + 1) * rows].astype(bf16)

    def target(self, k):
        return (self.o + k) % self.lines

    def over(self, k):
        return put(self.r.at[2 * self.target(k) + 1 - self.i], self.yb.at[k], self.snd.at[0], self.yrec.at[k], (self.d + 1 - 2 * self.i, self.m))

    def straight(self, k):
        return put(self.ys.at[k], self.z.at[k - 1], self.snd.at[1], self.zrec.at[k - 1], (self.target(k) * 2 + self.i, self.m))

    def start(self):
        for k in self.order:
            self.over(k).start()

    def fold(self, k):
        self.over(k).wait_recv()
        self.ys[k] = (self.r[2 * self.target(k) + self.i].astype(f32) + self.yb[k].astype(f32)).astype(bf16)
        if k:
            self.straight(k).start()

    def events(self):
        return [functools.partial(self.fold, k) for k in self.order]

    def finish(self):
        out = self.ys[0].astype(f32)
        for k in range(1, self.lines):
            self.straight(k).wait_recv()
            out = out + self.z[k - 1].astype(f32)
        for way, ref in ((0, self.r.at[pl.ds(0, self.lines)]), (1, self.ys.at[pl.ds(0, self.lines - 1)])):
            put(ref, ref, self.snd.at[way], self.zrec.at[0], (self.d, self.m)).wait_send()
        return out


class Queue:
    def __init__(self, items):
        self.items = list(items)

    def take(self, gaps):
        for _ in range(-(-len(self.items) // gaps)):
            self.items.pop(0)()


def layer_kernel(groups, weight, names, *refs):
    R = dict(zip(names, refs))

    class N:
        pass

    r = N()
    for key, ref in R.items():
        setattr(r, key, ref)
    micros, pairs = r.x0.shape[0], r.x0.shape[1]
    n = micros * pairs
    wins = pairs // WIN
    rows = r.sv.shape[0]
    tiles = r.enc.shape[0] // micros
    span = tiles * TILE
    steps = tiles + wins - 1
    total = 4 * groups
    lines = groups // 2
    d, m = lax.axis_index("dp"), lax.axis_index("mp")
    me = d * 4 + m
    xm, cm = flips(m)
    base = m * span

    for u in range(micros):
        for t in range(tiles):
            pltpu.make_async_copy(r.enc_hbm.at[u, pl.ds(base + t * TILE, TILE), :], r.enc.at[u * tiles + t], r.esem.at[u]).start()

    barrier = pltpu.get_barrier_semaphore()

    def hello(j, _):
        to = (me + j) % total
        pl.semaphore_signal(barrier, inc=1, device_id=(to // 4, to % 4), device_id_type=MESH)
        return 0

    lax.fori_loop(1, total, hello, 0)

    eye = (iota((rows, rows), 0) == iota((rows, rows), 1)).astype(bf16)

    def turned(x):
        return dot(eye, x, 1, 1).astype(bf16)

    def scaled(g, x):
        return (to_column(g.astype(f32)) * x.astype(f32)).astype(bf16)

    r.a1[m, d, :, 0:192] = scaled(r.g1[...], r.sv[...])
    r.a1[m, d, :, 192:384] = turned(r.so[...])
    r.a2[m, d, :, 0:192] = scaled(r.g2[...], r.wq[...])
    r.a2[m, d, :, 192:384] = r.wk[...]
    pl.semaphore_wait(barrier, total - 1)
    A1 = Spread(r.a1, (r.sa1, r.za1, r.ya1, r.xa1, r.ca1), wide=True)
    A2 = Spread(r.a2, (r.sa2, r.za2, r.ya2, r.xa2, r.ca2, r.qa2), wide=True, early=True)
    A3 = Spread(r.a3, (r.sa3, r.za3, r.ya3, r.xa3, r.ca3), wide=True)
    B1 = Spread(r.b1, (r.sb1, r.zb1, r.yb1))
    B2 = Spread(r.b2, (r.sb2, r.zb2, r.yb2))
    F = Spread(r.fd, (r.sf, r.zf, r.yf))
    A1.own()
    A2.own()
    r.b1[d] = scaled(r.g3[...], r.fi[...])
    r.a3[m, d, :, 0:192] = r.wv[...]
    r.a3[m, d, :, 192:384] = turned(r.co[...])
    r.b2[d] = r.fo[...]
    direction = r.dir1[...].astype(f32)
    own_dir = jnp.sum(jnp.where(iota((rows, D), 1) == d * rows + iota((rows, D), 0), direction, 0.0), axis=1, keepdims=True)
    r.fd[d] = fold_row(jnp.sum(own_dir * r.fo[...].astype(f32), axis=0, keepdims=True))

    for u in range(micros):
        def running(p, at, u=u):
            at = at + r.lens[u, 0, p]
            r.ends[u, p] = at
            return at
        lax.fori_loop(0, pairs, running, jnp.int32(0))
        w0 = jnp.int32(0)
        for w in range(wins):
            w0 = w0 + jnp.where(r.ends[u, WIN * w + WIN - 1] <= base, 1, 0)

        def stair(k, carry, u=u):
            t, w, live, pt, pw = carry
            r.tk[u, k] = t
            r.wk_[u, k] = w
            r.at[u, k] = jnp.where(live == 1, base + t * TILE, -(1 << 20))
            r.keepw[u, k] = jnp.where(w == pw, 1.0, 0.0)
            r.keept[u, k] = jnp.where(t == pt, 1.0, 0.0)
            wend, tend = r.ends[u, WIN * w + WIN - 1], base + (t + 1) * TILE
            nt = t + jnp.where(wend >= tend, 1, 0)
            nw = w + jnp.where(wend <= tend, 1, 0)
            on = live * jnp.where(nt < tiles, 1, 0)
            return jnp.where(on == 1, nt, t), jnp.minimum(jnp.where(on == 1, nw, w), wins - 1), on, t, w

        lax.fori_loop(0, steps, stair, (jnp.int32(0), jnp.minimum(w0, wins - 1), jnp.int32(1), jnp.int32(-1), jnp.int32(-1)))

        def last(table, out, count, u=u):
            def one(i, _):
                def scan(k, best):
                    return jnp.where(table[u, k] == i, k, best)
                out[u, i] = lax.fori_loop(0, steps, scan, jnp.int32(-1))
                return 0
            lax.fori_loop(0, count, one, 0)

        last(r.wk_, r.lw, wins)
        last(r.tk, r.lt, tiles)
    lens = jnp.concatenate([r.lensv[u].astype(f32) for u in range(micros)] + [jnp.zeros((8 - micros, pairs), f32)], axis=0)
    for w in range(wins):
        lane = iota((pairs, 128), 1)
        pair = WIN * w + lane % WIN
        stop = exact(lens, ((iota((pairs, 128), 0) <= pair) & (lane < COLS)).astype(f32))
        start = exact(lens, ((iota((pairs, 128), 0) < pair) & (lane < COLS)).astype(f32))
        for u in range(micros):
            r.hi[u, w] = stop[u:u + 1]
            r.lo[u, w] = start[u:u + 1]

    everyone = groups * pairs
    for g in range(groups):
        r.slotr[g:g + 1, :] = jnp.concatenate([r.slot[u:u + 1, g * pairs:(g + 1) * pairs] + u * everyone for u in range(micros)], axis=1)
    square = iota((n, n), 0) == iota((n, n), 1)
    slotc = jnp.sum(jnp.where(square, r.slotr[pl.ds(d, 1), :], 0), axis=1, keepdims=True)
    keyc = slotc // CAND

    for u in range(micros):
        part = r.enc.at[pl.ds(u * tiles, tiles)]
        pltpu.make_async_copy(part, part, r.esem.at[u]).wait()

    urgent = A1.events(2.0, 1.5) + A2.events(3.5, 1.5)
    last_one = max(t for t, _ in urgent)
    later = [(6.0, B1.own), (7.0, F.own), (9.0, A3.own)] + B1.events(9.0, 3.0) + F.events(11.0, 3.0) + A3.events(12.0, 2.0)
    events = sorted(urgent + later, key=lambda e: e[0])
    for t, e in events:
        if t <= last_one:
            e()
    A1.close()
    A2.close()
    queue = Queue(e for t, e in events if t > last_one)

    def weight_of(ref, k, c0):
        return ref[k, :, :, c0:c0 + WIDE].reshape(D, WIDE)

    G0 = Reduce(r.r0, r.yr0, r.ys0, r.z0, (r.snd0, r.yrec0, r.zrec0))
    GV = Reduce(r.r2, r.yr2, r.ys2, r.z2, (r.snd2, r.yrec2, r.zrec2))
    def halve(src, buf, mid, fin, ss, rs):
        xcm = (cm + 2) % 4
        near = [put(src.at[cm], buf.at[0], ss.at[0], rs.at[0], (d, cm)), put(src.at[xcm], buf.at[1], ss.at[1], rs.at[1], (d, cm))]
        far = put(mid, fin, ss.at[2], rs.at[2], (d, xm))

        def one():
            for c in near:
                c.start()

        def two():
            for c in near:
                c.wait()
            mid[...] = (src[xm].astype(f32) + buf[1].astype(f32)).astype(bf16)
            far.start()

        def three():
            far.wait()
            return src[m].astype(f32) + buf[0].astype(f32) + fin[...].astype(f32)

        return one, two, three

    chunks = ((0, 7), (7, 13), (13, steps))

    def attention(chain, acc):
        r.chain, r.acc = chain, acc
        x0 = r.x0[...].reshape(n, D).astype(f32)
        y1b = rms(x0)[0].astype(bf16)
        x1 = x0
        for k in range(4):
            v1 = dot(y1b, weight_of(r.a1, k, 0)).astype(bf16)
            r.v1[k] = v1
            x1 = x1 + dot(v1, weight_of(r.a1, k, 192), 1, 1)
        r.x1[...] = x1
        y2b = rms(x1)[0].astype(bf16)

        def fill_windows(k, value):
            for j in range(PER):
                h = PER * k + j
                r.chain[0:micros * wins, h * WIN:(h + 1) * WIN, :] = value[j * n:(j + 1) * n].reshape(micros * wins, WIN, D)

        gap = jnp.zeros((micros, wins, 128 - COLS, D), bf16)
        for k in range(4):
            q = dot(y2b, weight_of(r.a2, k, 0)).astype(bf16)
            r.q[k] = q
            fill_windows(k, dot(expand(q), weight_of(r.a2, k, 192), 1, 1))
        r.qu[:, :, 0:COLS, :] = r.chain[0:micros * wins].astype(bf16).reshape(micros, wins, COLS, D)
        r.qu[:, :, COLS:128, :] = gap
        r.qu[:, :, 128 + COLS:256, :] = gap

        gaps = 2 * micros * len(chunks)

        def tile_rows(u, k):
            return r.enc[u * tiles + r.tk[u, k]]

        line = iota((TILE, 128), 0).astype(f32)
        for u in range(micros):
            def scores(k, u=u):
                w = r.wk_[u, k]
                s = dot(tile_rows(u, k), r.qu[u, w, 0:128, :], 1, 1)
                at = line + r.at[u, k].astype(f32)
                s = jnp.where((at >= r.lo[u, w]) & (at < r.hi[u, w]), s, FAR)
                high = s.astype(bf16)
                r.da[u, k, :, 0:128] = high
                r.da[u, k, :, 128:256] = (s - high.astype(f32)).astype(bf16)
                r.sm[k] = jnp.max(s, axis=0, keepdims=True)

            for a, b in chunks:
                loop(a, b, scores)
                queue.take(gaps)
                gaps -= 1
            for w in range(wins):
                top = jnp.full((1, 128), FAR, f32)
                for k in range(steps):
                    top = jnp.where(jnp.full((1, 128), r.wk_[u, k]) == w, jnp.maximum(top, r.sm[k]), top)
                r.mw[u, w] = top

            def weights(k, u=u):
                w = r.wk_[u, k]
                s = r.da[u, k, :, 0:128].astype(f32) + r.da[u, k, :, 128:256].astype(f32)
                p = jnp.where(s > 0.5 * FAR, jnp.exp(s - r.mw[u, w]), 0.0)
                r.sm[k] = jnp.sum(p, axis=0, keepdims=True)
                low = p.astype(bf16)
                r.da[u, k, :, 128:256] = low
                acc = dot(low, tile_rows(u, k), 0, 0)[0:COLS] + r.acc[0:COLS] * r.keepw[u, k]
                r.acc[0:COLS] = acc
                r.chain[k] = acc

            r.acc[...] = jnp.zeros_like(r.acc)
            for a, b in chunks:
                loop(a, b, weights)
                queue.take(gaps)
                gaps -= 1
            for w in range(wins):
                tot = jnp.zeros((1, 128), f32)
                for k in range(steps):
                    tot = jnp.where(jnp.full((1, 128), r.wk_[u, k]) == w, tot + r.sm[k], tot)
                r.lw_[u, w] = tot
            inv = to_pairs(r.lw_[u].reshape(wins, 128))
            inv = jnp.where(inv > 0.0, 1.0 / jnp.where(inv > 0.0, inv, 1.0), 0.0)
            for h in range(HEADS):
                parts = []
                for w in range(wins):
                    k = r.lw[u, w]
                    part = r.chain[jnp.maximum(k, 0), h * WIN:(h + 1) * WIN, :]
                    scale = inv[w * WIN:(w + 1) * WIN, h:h + 1]
                    parts.append(jnp.where(scale > 0.0, part * scale, 0.0))
                r.c[h, u * pairs:(u + 1) * pairs, :] = jnp.concatenate(parts, axis=0).astype(bf16)
        while queue.items:
            queue.take(1)
        A3.close()
        B2.own()
        mx = to_pairs(r.mw[...].reshape(micros * wins, 128))
        lx = to_pairs(r.lw_[...].reshape(micros * wins, 128))
        some = lx > 0.0
        lse_own = jnp.where(some, mx + jnp.log(jnp.where(some, lx, 1.0)), FAR)
        r.mx[...] = mx
        r.lown[...] = lse_own
        own = []
        for k in range(4):
            ctx = collapse(dot(r.c[PER * k:PER * (k + 1)].reshape(PER * n, D), weight_of(r.a3, k, 0)), n)
            own.append(ctx)
        fill(r.csend, own)
        hop = [put(r.csend, r.cbuf0, r.csem.at[0], r.crec.at[0], (d, cm)), put(r.lown, r.lbuf.at[0], r.csem.at[1], r.crec.at[1], (d, cm))]
        for c in hop:
            c.start()
        fd = r.fd[0]
        for g in range(1, groups):
            fd = fd + r.fd[g]
        fd = unfold_row(fd)
        for c in hop:
            c.wait()
        both, lse = merge(own, lse_own, blocks(r.cbuf0), r.lbuf[0])
        fill(r.cmid, both)
        r.lmid[...] = lse
        hop = [put(r.cmid, r.cbuf1, r.csem.at[2], r.crec.at[2], (d, xm)), put(r.lmid, r.lbuf.at[1], r.csem.at[3], r.crec.at[3], (d, xm))]
        for c in hop:
            c.start()
        for c in hop:
            c.wait()
        both, lse = merge(both, lse, blocks(r.cbuf1), r.lbuf[1])
        r.lse[...] = lse
        x2 = r.x1[...]
        for k in range(4):
            low = both[k].astype(bf16)
            r.ctx[k] = low
            x2 = x2 + dot(low, weight_of(r.a3, k, 192), 1, 1)
        ffi = r.b1[...].reshape(D, D)
        y3, r3 = rms(x2)
        y3b = y3.astype(bf16)
        act, slope = gelu(dot(y3b, ffi))
        hid = act.astype(bf16)
        hidf = hid.astype(f32)
        score = jnp.sum(hidf * fd, axis=1, keepdims=True) + jnp.where(m == 0, jnp.sum(x2 * direction, axis=1, keepdims=True), 0.0)
        rel = jnp.concatenate([r.rel[u:u + 1, :] for u in range(micros)], axis=1)
        which = iota((8, n), 0)
        r.msgs[0] = jnp.where(which == 0, to_row(score), jnp.where(which == 1, rel, 0.0))

        def tell(j, _):
            to = (me + j) % total
            put(r.msgs.at[0], r.msgs.at[total - j], r.msem.at[0], r.msem.at[1], (to // 4, to % 4)).start()
            return 0

        lax.fori_loop(1, total, tell, 0)
        r.hid[...] = hid
        r.x3[...] = x2.reshape(micros, pairs, D)

        heard = r.msgs.at[pl.ds(1, total - 1)]
        put(heard, heard, r.msem.at[0], r.msem.at[1], (d, cm)).wait()
        lane = iota((1, n), 1)

        def rows_of(g):
            four = [r.msgs[(4 * g + k - me + total) % total] for k in range(4)]
            s = (four[0] + four[1] + four[2] + four[3])[0:1]
            slot = (lane // pairs) * everyone + g * pairs + lane % pairs
            mine = r.slotr[pl.ds(g, 1), :]
            return s, four[0][1:2], mine // CAND == keyc, mine == slotc, slot // CAND == keyc, slot == slotc

        def tops(g, carry):
            a, b, own, rown = carry
            s, rel, same, mine, rsame, rmine = rows_of(g)
            return (jnp.maximum(a, jnp.where(same, s, FAR)), jnp.maximum(b, jnp.where(rsame, rel, FAR)),
                    own + jnp.where(mine, s, 0.0), rown + jnp.where(rmine, rel, 0.0))

        z = jnp.zeros((n, n), f32)
        far = jnp.full((n, n), FAR, f32)
        a, b, sown, rown = lax.fori_loop(0, groups, tops, (far, far, z, z), unroll=groups <= 8)
        a, b = jnp.max(a, axis=1, keepdims=True), jnp.max(b, axis=1, keepdims=True)
        sown, rown = jnp.sum(sown, axis=1, keepdims=True), jnp.sum(rown, axis=1, keepdims=True)

        def sums(g, carry):
            s, rel, same, _, rsame, _ = rows_of(g)
            return (carry[0] + jnp.where(same, jnp.exp(s - a), 0.0), carry[1] + jnp.where(rsame, jnp.exp(rel - b), 0.0))

        sa, sb = lax.fori_loop(0, groups, sums, (z, z), unroll=groups <= 8)
        dscore = weight * (jnp.exp(sown - a) / jnp.sum(sa, axis=1, keepdims=True) - jnp.exp(rown - b) / jnp.sum(sb, axis=1, keepdims=True))
        du = (slope * dscore * fd).astype(bf16)
        dn3p = dot(du, ffi, 1, 1)
        r.nmid[0] = dn3p.astype(bf16)
        nhop = put(r.nmid.at[0], r.nbuf.at[0], r.nsem.at[0], r.nrec.at[0], (d, cm))
        nhop.start()
        r.hsum[0] = fold_row(jnp.sum(hidf * dscore, axis=0, keepdims=True))

        def scatter(j, _):
            to = (d + j) % groups
            put(r.hsum.at[0], r.hsum.at[groups - j], r.hsem.at[0], r.hsem.at[1], (to, m)).start()
            return 0

        nhop.wait()
        part = dn3p + r.nbuf[0].astype(f32)
        r.nmid[1] = part.astype(bf16)
        nhop = put(r.nmid.at[1], r.nbuf.at[1], r.nsem.at[1], r.nrec.at[1], (d, xm))
        nhop.start()
        lax.fori_loop(1, groups, scatter, 0)
        gff = dot(y3b, du, 0, 0)
        nhop.wait()
        dn3 = part + r.nbuf[1].astype(f32)
        dx2 = dscore * direction + norm_back(y3, r3, dn3)
        r.dx2[...] = dx2
        gc = dx2.astype(bf16)
        delta = jnp.zeros((n, 128), f32)
        for k in range(4):
            dctx = dot(gc, weight_of(r.a3, k, 192)).astype(bf16)
            r.dctx[k] = dctx
            pick = (iota((WIDE, 128), 0) // HEAD + PER * k == iota((WIDE, 128), 1)).astype(f32)
            delta = delta + exact(dctx.astype(f32) * both[k], pick)
        ones = jnp.ones((n, 64), bf16)
        G0.fill(jnp.concatenate([gff, dot(gc, r.ctx[m], 0, 0), dot((dn3 * y3).astype(bf16), ones, 0, 0)], axis=1))
        G0.start()
        r.alpha[...] = to_windows(jnp.exp(jnp.minimum(r.mx[...] - lse, 1.0))).reshape(r.alpha.shape)
        r.delta[...] = to_windows(delta).reshape(r.delta.shape)
        share = jnp.exp(jnp.minimum(r.lown[...] - lse, 1.0))
        for k in range(4):
            dctx = expand(r.dctx[k])
            fill_windows(k, dot(dctx, weight_of(r.a3, k, 0), 1, 1))
            spread = jnp.concatenate([dctx[j * n:(j + 1) * n] * share[:, PER * k + j:PER * k + j + 1].astype(bf16) for j in range(PER)], axis=0)
            r.g[k] = dot(r.c[PER * k:PER * (k + 1)].reshape(PER * n, D), spread, 0, 0).astype(bf16)
        r.qu[:, :, 128:128 + COLS, :] = r.chain[0:micros * wins].astype(bf16).reshape(micros, wins, COLS, D)

        v_one, v_two, v_three = halve(r.g, r.gvb, r.gvm, r.gvf, r.vsem, r.vrec)
        v_one()

        def value_out():
            GV.fill(jnp.concatenate([v_three(), jnp.zeros((D, 64), f32)], axis=1))
            GV.start()

        queue.items = [v_two] + G0.events() + [value_out] + [e for _, e in sorted(B2.events(0.0, 1.0), key=lambda e: e[0])] + GV.events()
        gaps = micros * len(chunks) + 3

        def back(k, u):
            w = r.wk_[u, k]
            tile = tile_rows(u, k)
            da = dot(tile, r.qu[u, w, 128:256, :], 1, 1)
            a = r.da[u, k, :, 128:256].astype(f32) * r.alpha[u, w]
            ds = (a * (da - r.delta[u, w])).astype(bf16)
            r.da[u, k, :, 0:128] = ds
            r.da[u, k, :, 128:256] = a.astype(bf16)
            acc = dot(ds, tile, 0, 0)[0:COLS] + r.acc[0:COLS] * r.keepw[u, k]
            r.acc[0:COLS] = acc
            r.chain[k] = acc

        for u in range(micros):
            r.acc[...] = jnp.zeros_like(r.acc)
            for a, b in chunks:
                loop(a, b, lambda k, u=u: back(k, u))
                queue.take(gaps)
                gaps -= 1
            for h in range(HEADS):
                parts = []
                for w in range(wins):
                    k = r.lw[u, w]
                    parts.append(jnp.where(jnp.full((WIN, D), k) >= 0, r.chain[jnp.maximum(k, 0), h * WIN:(h + 1) * WIN, :], 0.0))
                r.c[h, u * pairs:(u + 1) * pairs, :] = jnp.concatenate(parts, axis=0).astype(bf16)

    pl.run_scoped(attention, pltpu.VMEM((steps, COLS, D), f32), pltpu.VMEM((128, D), f32))

    def rest_of_it(r1, ys1, full, out):
        r.r1, r.ys1, r.full, r.out = r1, ys1, full, out
        G1 = Reduce(r.r1, r.yr1, r.ys1, r.z1, (r.snd1, r.yrec1, r.zrec1))
        part = [collapse(dot(r.c[PER * k:PER * (k + 1)].reshape(PER * n, D), weight_of(r.a2, k, 192)), n) for k in range(4)]
        fill(r.csend, part)
        hop = put(r.csend, r.cbuf0, r.qsem.at[0], r.qrec.at[0], (d, cm))
        hop.start()
        for k in range(4):
            r.g[k] = dot(r.c[PER * k:PER * (k + 1)].reshape(PER * n, D), expand(r.q[k]), 0, 0).astype(bf16)
        k_one, k_two, k_three = halve(r.g, r.gkb, r.gvm, r.gkf, r.ksem, r.krec)
        hop.wait()
        part = [x + y.astype(f32) for x, y in zip(part, blocks(r.cbuf0))]
        fill(r.cmid, part)
        hop = put(r.cmid, r.cbuf1, r.qsem.at[1], r.qrec.at[1], (d, xm))
        hop.start()
        k_one()
        while queue.items:
            queue.take(1)
        x3p = dot(r.hid[...], r.b2[...].reshape(D, D), 1, 1)
        r.nmid[0] = x3p.astype(bf16)
        xhop = put(r.nmid.at[0], r.nbuf.at[0], r.xsem.at[0], r.xrec.at[0], (d, cm))
        xhop.start()
        x1 = r.x1[...]
        y1, g1 = rms(r.x0[...].reshape(n, D).astype(f32))
        y2, g2 = rms(x1)
        k_two()
        hop.wait()
        dn2 = 0
        for k in range(4):
            dq = (part[k] + blocks(r.cbuf1)[k].astype(f32)).astype(bf16)
            r.dq[k] = dq
            dn2 = dn2 + dot(dq, weight_of(r.a2, k, 0), 1, 1)
        dx1 = r.dx2[...] + norm_back(y2, g2, dn2)
        gs = dx1.astype(bf16)
        dn1 = 0
        for k in range(4):
            dv = dot(gs, weight_of(r.a1, k, 192)).astype(bf16)
            r.dctx[k] = dv
            dn1 = dn1 + dot(dv, weight_of(r.a1, k, 0), 1, 1)
        r.dx0[...] = (dx1 + norm_back(y1, g1, dn1)).reshape(micros, pairs, D)
        ones = jnp.ones((n, 64), bf16)
        half_ones = jnp.where(iota((n, 64), 1) < 32, ones, 0)
        small = [dot(y1.astype(bf16), r.dctx[m], 0, 0), dot(gs, r.v1[m], 0, 0), dot(y2.astype(bf16), r.dq[m], 0, 0)]
        tail = dot((dn1 * y1).astype(bf16), half_ones, 0, 0) + dot((dn2 * y2).astype(bf16), ones - half_ones, 0, 0)
        G1.fill(jnp.concatenate(small + [k_three(), tail, jnp.zeros((D, 64), f32)], axis=1))
        G1.start()
        xhop.wait()
        x3p = x3p + r.nbuf[0].astype(f32)
        r.nmid[1] = x3p.astype(bf16)
        xhop = put(r.nmid.at[1], r.nbuf.at[1], r.xsem.at[1], r.xrec.at[1], (d, xm))
        xhop.start()
        queue.items += G1.events()
        gaps = micros * 4

        def rows_out(u, t, slot):
            return pltpu.make_async_copy(r.out.at[slot], r.de.at[u, pl.ds(t * TILE, TILE), :], r.osem.at[slot])

        for u in range(micros):
            if u == 0:
                r.full[...] = jnp.zeros_like(r.full)
            for a, b in ((0, 10), (10, steps)):
                loop(a, b, functools.partial(place, r, u))
                queue.take(gaps)
                gaps -= 1
            for t in range(tiles):
                slot = (u * tiles + t) % OUTS
                if u * tiles + t >= OUTS:
                    rows_out(u, t, slot).wait()
                k = jnp.maximum(r.lt[u, t], 0)
                r.out[slot] = r.enc[k]
                rows_out(u, t, slot).start()
                if t % 6 == 5:
                    queue.take(gaps)
                    gaps -= 1
        for slot in range(OUTS):
            rows_out(micros - 1, tiles - 1, slot).wait()
        while queue.items:
            queue.take(1)

        heard = r.hsum.at[pl.ds(1, groups - 1)]
        put(heard, heard, r.hsem.at[0], r.hsem.at[1], (d, cm)).wait()
        total_h = r.hsum[0]
        for g in range(1, groups):
            total_h = total_h + r.hsum[g]
        r.hs[...] = total_h
        xhop.wait()
        r.x3[...] = r.x3[...] + (x3p + r.nbuf[1].astype(f32)).reshape(micros, pairs, D)
        r.out0[...] = G0.finish()
        r.out2[...] = GV.finish()
        r.out1[...] = G1.finish()

    pl.run_scoped(rest_of_it, pltpu.VMEM((groups, rows, 896), bf16), pltpu.VMEM((lines, rows, 896), bf16), pltpu.VMEM((TILE, D), f32), pltpu.VMEM((OUTS, TILE, D), bf16))
    for part in (A1, A2, A3, B1, B2, F):
        part.sent()


def place(r, u, k):
    acc = dot(r.da[u, k], r.qu[u, r.wk_[u, k]]) + r.full[...] * r.keept[u, k]
    r.full[...] = acc
    r.enc[k] = acc.astype(bf16)


def layer(groups, weight, x0, encoded, lens, slot, rel, dir1, g1, g2, g3, sv, so, wq, wk, wv, co, fi, fo):
    micros, pairs = x0.shape[0], x0.shape[1]
    n, wins, rows, lines = micros * pairs, pairs // WIN, sv.shape[0], groups // 2
    span = encoded.shape[1] // 4
    tiles = span // TILE
    steps = tiles + wins - 1
    sd = jax.ShapeDtypeStruct
    any_, vm, sm = (pl.BlockSpec(memory_space=s) for s in (pl.ANY, pltpu.VMEM, pltpu.SMEM))
    S, V, M = pltpu.SemaphoreType.DMA, pltpu.VMEM, pltpu.SMEM
    ins = dict(x0=x0, enc_hbm=encoded, lens=lens, lensv=lens, slot=slot, rel=rel, dir1=dir1, g1=g1, g2=g2, g3=g3,
               sv=sv, so=so, wq=wq, wk=wk, wv=wv, co=co, fi=fi, fo=fo)
    places = dict(enc_hbm=any_, lens=sm)
    outs = dict(x3=sd((micros, pairs, D), f32), dx0=sd((micros, pairs, D), f32), de=sd((micros, span, D), bf16), hs=sd((8, 128), f32),
                out0=sd((rows, 1024), f32), out1=sd((rows, 896), f32), out2=sd((rows, 256), f32))
    places.update(de=any_)
    scratch = dict(
        enc=V((max(micros * tiles, steps), TILE, D), bf16), esem=S((micros,)),
        a1=V((4, groups, rows, 384), bf16), a2=V((4, groups, rows, 384), bf16), a3=V((4, groups, rows, 384), bf16),
        b1=V((groups, rows, D), bf16), b2=V((groups, rows, D), bf16), fd=V((groups, 8, 128), f32), hid=V((n, D), bf16),
        ends=M((micros, pairs), jnp.int32), tk=M((micros, steps), jnp.int32), wk_=M((micros, steps), jnp.int32), at=M((micros, steps), jnp.int32),
        keepw=M((micros, steps), f32), keept=M((micros, steps), f32), lw=M((micros, wins), jnp.int32), lt=M((micros, tiles), jnp.int32),
        lo=V((micros, wins, 1, 128), f32), hi=V((micros, wins, 1, 128), f32), slotr=V((groups, n), jnp.int32),
        x1=V((n, D), f32), v1=V((4, n, WIDE), bf16), q=V((4, n, WIDE), bf16), qu=V((micros, wins, 256, D), bf16), sm=V((steps, 1, 128), f32), mw=V((micros, wins, 1, 128), f32), lw_=V((micros, wins, 1, 128), f32),
        da=V((micros, steps, TILE, 256), bf16), c=V((HEADS, n, D), bf16), mx=V((n, 128), f32), lown=V((n, 128), f32), lse=V((n, 128), f32),
        csend=V((2, n, 384), bf16), cmid=V((2, n, 384), bf16), cbuf0=V((2, n, 384), bf16), cbuf1=V((2, n, 384), bf16), lmid=V((n, 128), f32), lbuf=V((2, n, 128), f32),
        csem=S((4,)), crec=S((4,)), ctx=V((4, n, WIDE), bf16), msgs=V((4 * groups, 8, n), f32), msem=S((2,)),
        xsem=S((2,)), xrec=S((2,)), nmid=V((2, n, D), bf16), nbuf=V((2, n, D), bf16), nsem=S((2,)), nrec=S((2,)),
        hsum=V((groups, 8, 128), f32), hsem=S((2,)), dx2=V((n, D), f32), dctx=V((4, n, WIDE), bf16), dq=V((4, n, WIDE), bf16),
        alpha=V((micros, wins, 1, 128), f32), delta=V((micros, wins, 1, 128), f32),
        g=V((4, D, WIDE), bf16), gvb=V((2, D, WIDE), bf16), gvm=V((D, WIDE), bf16), gvf=V((D, WIDE), bf16), vsem=S((3,)), vrec=S((3,)),
        gkb=V((2, D, WIDE), bf16), gkf=V((D, WIDE), bf16), ksem=S((3,)), krec=S((3,)), qsem=S((2,)), qrec=S((2,)),
        osem=S((OUTS,)),
    )
    for part in ("a1", "a2", "a3", "b1", "b2", "f"):
        scratch.update({"s" + part: S((5,)), "z" + part: S((lines,)), "y" + part: S((lines,))})
        if part[0] == "a":
            scratch.update({"x" + part: S((groups,)), "c" + part: S((2,)), "q" + part: S((lines,))})
    for tag, columns in (("0", 1024), ("1", 896), ("2", 256)):
        piece = lambda k: V((k, rows, columns), bf16)
        if tag != "1":
            scratch.update({"r" + tag: piece(groups), "ys" + tag: piece(lines)})
        scratch.update({"yr" + tag: piece(lines), "z" + tag: piece(lines - 1),
                        "snd" + tag: S((2,)), "yrec" + tag: S((lines,)), "zrec" + tag: S((lines - 1,))})
    names = tuple(ins) + tuple(outs) + tuple(scratch)
    return pl.pallas_call(
        functools.partial(layer_kernel, groups, weight, names),
        out_shape=tuple(outs.values()),
        in_specs=[places.get(k, vm) for k in ins], out_specs=[places.get(k, vm) for k in outs],
        scratch_shapes=list(scratch.values()),
        compiler_params=pltpu.CompilerParams(collective_id=0, has_side_effects=True, vmem_limit_bytes=VMEM),
        name="decoder_layer",
    )(*ins.values())


def outputs_kernel(dir_ref, hs, out0, out1, out2, g1, g2, g3, x3, dx0, de,
                   g_self, g_cross, g_ff, self_value, self_out, query, key, value, cross_out, ff_in, ff_out, x3_out, dx0_out, de_out, room, sem):
    parts = de.shape[1] // 768
    every = [(u, pl.ds(k * 768, 768), u * parts + k) for u in range(de.shape[0]) for k in range(parts)]
    loads = [pltpu.make_async_copy(de.at[u, at], room.at[k], sem.at[0, k]) for u, at, k in every]
    stores = [pltpu.make_async_copy(room.at[k], de_out.at[u, at], sem.at[1, k]) for u, at, k in every]
    for c in loads:
        c.start()
    rows = out0.shape[0]
    columns = [to_column(g[...].astype(f32)) for g in (g1, g2, g3)]
    g_self[...] = to_row(out1[:, 768:769] / columns[0])
    g_cross[...] = to_row(out1[:, 800:801] / columns[1])
    g_ff[...] = to_row(out0[:, 960:961] / columns[2])
    self_value[...] = out1[:, 0:192] * columns[0]
    self_out[...] = out1[:, 192:384].T
    query[...] = out1[:, 384:576] * columns[1]
    key[...] = out1[:, 576:768]
    value[...] = out2[:, 0:192]
    cross_out[...] = out0[:, 768:960].T
    ff_in[...] = out0[:, 0:768] * columns[2]
    mine = iota((rows, D), 1) == lax.axis_index("dp") * rows + iota((rows, D), 0)
    own_dir = jnp.sum(jnp.where(mine, dir_ref[...].astype(f32), 0.0), axis=1, keepdims=True)
    ff_out[...] = own_dir * unfold_row(hs[...])
    x3_out[...] = x3[...]
    dx0_out[...] = dx0[...]
    for c, back in zip(loads, stores):
        c.wait()
        back.start()
    for c in stores:
        c.wait()


def outputs(dir1, hs, out0, out1, out2, g1, g2, g3, x3, dx0, de):
    rows, count = out0.shape[0], de.shape[0] * de.shape[1] // 768
    sd = jax.ShapeDtypeStruct
    tall, flat = sd((rows, WIDE), f32), sd((WIDE, rows), f32)
    any_, vm = (pl.BlockSpec(memory_space=s) for s in (pl.ANY, pltpu.VMEM))
    return pl.pallas_call(
        outputs_kernel,
        out_shape=(sd((1, rows), f32),) * 3 + (tall, flat, tall, tall, tall, flat, sd((rows, D), f32), sd((rows, D), f32),
                                               sd(x3.shape, f32), sd(x3.shape, f32), sd(de.shape, bf16)),
        in_specs=[vm] * 10 + [any_], out_specs=[vm] * 13 + [any_],
        scratch_shapes=[pltpu.VMEM((count, 768, D), bf16), pltpu.SemaphoreType.DMA((2, count))],
        compiler_params=pltpu.CompilerParams(vmem_limit_bytes=32 << 20),
        name="outputs",
    )(dir1, hs, out0, out1, out2, g1, g2, g3, x3, dx0, de)


def shards(dec_in, encoded, seg_lengths, pair_slot, relevance, score_dir, gain_self, gain_cross, gain_ff,
           self_value, self_out, cross_query, cross_key, cross_value, cross_out, ff_in, ff_out):
    groups = lax.axis_size("dp")
    gains = [g.reshape(1, -1) for g in (gain_self, gain_cross, gain_ff)]
    dir1 = score_dir.reshape(1, D)
    x3, dx0, d_encoded, hs, out0, out1, out2 = layer(
        groups, CAND * math.sqrt(D), dec_in, encoded, seg_lengths, pair_slot, relevance, dir1, *gains,
        self_value, self_out, cross_query, cross_key, cross_value, cross_out, ff_in, ff_out.T)
    g1, g2, g3, *weights, x3, dx0, d_encoded = outputs(dir1, hs, out0, out1, out2, *gains, x3, dx0, d_encoded)
    weights[-1] = weights[-1].T
    return (x3, dx0, d_encoded, g1.reshape(-1), g2.reshape(-1), g3.reshape(-1), *weights)


def solution(mesh):
    in_specs = (
        P(None, "dp", None),
        P(None, "dp", None),
        P(None, "dp", None),
        P(),
        P(None, "dp"),
        P(),
        P("dp"),
        P("dp"),
        P("dp"),
        P("dp", "mp"),
        P("mp", "dp"),
        P("dp", "mp"),
        P("dp", "mp"),
        P("dp", "mp"),
        P("mp", "dp"),
        P("dp", "mp"),
        P("mp", "dp"),
    )
    out_specs = (
        P(None, "dp", None),
        P(None, "dp", None),
        P(None, ("dp", "mp"), None),
        P("dp"),
        P("dp"),
        P("dp"),
        P("dp", "mp"),
        P("mp", "dp"),
        P("dp", "mp"),
        P("dp", "mp"),
        P("dp", "mp"),
        P("mp", "dp"),
        P("dp", "mp"),
        P("mp", "dp"),
    )
    return jax.shard_map(shards, mesh=mesh, in_specs=in_specs, out_specs=out_specs, check_vma=False)
```

time: 1230 us -> 201 us (0.16)
  waiting for transfers between devices: 493 us -> 0 us
  blocking collectives: 250 us -> 0 us
  matrix products: 216 us -> 0 us
  Pallas kernels: 0 us -> 190 us
  other arithmetic: 129 us -> 0 us
  local copies, waits for them, and re-layouts: 70.2 us -> 10.5 us
  starting transfers between devices: 41.9 us -> 0 us
  between operations: 18.6 us -> 0.88 us
    dot_general x52 -> x0, matrix products: 216 us -> none  [product(): return jnp.einsum(form, left, right, preferred_element_type=jnp.float32)]
    reduce_scatter x4 -> x0, waiting for transfers between devices: 210 us -> none  [the longest x1 72.2 us: shards(): lax.psum_scatter(local_grads[10], 'dp', scatter_dimension=1, tiled=True)]
    all_gather x6 -> x0, blocking collectives: 190 us -> none  [the longest x1 33.1 us: fetch(): lax.all_gather(cross_value, 'dp', axis=0, tiled=True)]
    pallas_call x0 -> x2, Pallas kernels: none -> 190 us  [the longest x1 182 us: layer(): pl.pallas_call(functools.partial(layer_kernel, groups, weight, names), ou...]
    all_to_all x8 -> x0, waiting for transfers between devices: 114 us -> none  [the longest x2 64 us: shards(): lax.all_to_all(grad_key, 'mp', split_axis=0, concat_axis=1, tiled=True)]
    psum x6 -> x0, waiting for transfers between devices: 92.9 us -> none  [head_total(): return lax.psum(partial_value, 'mp')]
    unnamed x2 -> x0, blocking collectives: 59.8 us -> none
    all_gather x4 -> x0, waiting for transfers between devices: 47.6 us -> none  [the longest x1 40.5 us: fetch(): lax.all_gather(ff_out, 'dp', axis=1, tiled=True)]
  transfers between devices with their start and end apart: 26 -> 0, of which waited for: 15 -> 0; matrix products, arithmetic and copies ran while one was open for 18% -> 0% of each run, Pallas kernels for 0% -> 0%
where the time goes in v2:
time: 201 us
  Pallas kernels  190 us (95%)
  local copies, waits for them, and re-layouts  10.5 us (5%)
    pallas_call x1, Pallas kernels, layer(): pl.pallas_call(functools.partial(layer_kernel, groups, weight, names), ou...  182 us
    unnamed x22, local copies, waits for them, and re-layouts  9.22 us
    pallas_call x1, Pallas kernels, outputs(): pl.pallas_call(outputs_kernel, out_shape=(sd((1, rows), f32),) * 3 + (tal...  7.46 us

profile of v2, /device:TPU:0, one launch (start us, length us, event | category | flops | bytes accessed | tf_op | source)
XLA Modules:
  0.0 200.9 jit_solution(10649125063326087120)
XLA Ops:
  0.6 1.3 reshape.49.refs_6_.dir_ref
  1.9 0.0 copy-start.6
  1.9 0.0 copy-start.8
  1.9 0.0 copy-start.9
  1.9 0.0 copy-start.10
  1.9 182.1 %decoder_layer.1 = (f32[2,64,768]{2,1,0:T(8,128)}, f32[2,64,768]{2,1,0:T(8,128)}, bf16[2,3072,768]{2,1,0:T(8,128)(2,1)}, f32[8,128]{1,0:T(8,128)}, f32[96,1024]{...) custom-call(bf16[2,64,768]{2,1,0:T(8,128)(2,1)} %refs_0_.1, bf16[2,12288,768]{2,1,0:T(8,128)(2,1)} %refs_1_.1, ...), custom_call_target="tpu_custom_call" | custom-call | tf_op jit(solution)/shard_map/decoder_layer/pallas_call | solution.py:854
  184.0 0.0 copy-done.6
  184.0 0.0 copy-done.8
  184.0 0.0 copy-done.9
  184.1 0.0 copy-done.10
  184.1 0.0 copy-start
  184.1 3.7 %copy-done = bf16[2,3072,768]{2,1,0:T(8,128)(2,1)S(1)} copy-done((bf16[2,3072,768]{2,1,0:T(8,128)(2,1)S(1)}, bf16[2,3072,768]{2,1,0:T(8,128)(2,1)}, u32[]{:S(2)}) %copy-start) | copy-done | bytes 9437208
  187.8 0.0 copy-start.1
  187.8 1.0 copy-done.1
  188.7 0.0 copy-start.2
  188.7 1.0 copy-done.2
  189.7 0.0 copy-start.3
  189.7 1.0 copy-done.3
  190.7 0.0 copy-start.4
  190.7 1.0 copy-done.4
  191.7 0.0 copy-start.5
  191.7 0.9 copy-done.5
  192.6 0.0 copy-start.7
  192.6 0.7 copy-done.7
  193.3 7.5 %outputs.1 = (f32[1,96]{1,0:T(1,128)}, f32[1,96]{1,0:T(1,128)}, f32[1,96]{1,0:T(1,128)}, f32[96,192]{1,0:T(8,128)}, f32[192,96]{1,0:T(8,128)}, /*index=5*/f32[96...) custom-call(bf16[1,768]{1,0:T(2,128)(2,1)S(1)} %copy-done.6, ...), custom_call_target="tpu_custom_call" | custom-call | tf_op jit(solution)/shard_map/outputs/pallas_call | solution.py:901
Async XLA Ops:
  1.9 182.1 %copy-start.6 = (bf16[1,768]{1,0:T(2,128)(2,1)S(1)}, bf16[1,768]{1,0:T(2,128)(2,1)}, u32[]{:S(2)}) copy-start(bf16[1,768]{1,0:T(2,128)(2,1)} %reshape.49.refs_6_.dir_ref) | copy-start | bytes 4612
  1.9 182.1 %copy-start.8 = (bf16[96]{0:T(256)(128)(2,1)S(1)}, bf16[96]{0:T(256)(128)(2,1)}, u32[]{:S(2)}) copy-start(bf16[96]{0:T(256)(128)(2,1)} %param.23) | copy-start | bytes 580
  1.9 182.1 %copy-start.9 = (bf16[96]{0:T(256)(128)(2,1)S(1)}, bf16[96]{0:T(256)(128)(2,1)}, u32[]{:S(2)}) copy-start(bf16[96]{0:T(256)(128)(2,1)} %param.24) | copy-start | bytes 580
  1.9 182.1 %copy-start.10 = (bf16[96]{0:T(256)(128)(2,1)S(1)}, bf16[96]{0:T(256)(128)(2,1)}, u32[]{:S(2)}) copy-start(bf16[96]{0:T(256)(128)(2,1)} %param.25) | copy-start | bytes 580
  184.1 3.7 %copy-start = (bf16[2,3072,768]{2,1,0:T(8,128)(2,1)S(1)}, bf16[2,3072,768]{2,1,0:T(8,128)(2,1)}, u32[]{:S(2)}) copy-start(bf16[2,3072,768]{2,1,0:T(8,128)(2,1)} %get-tuple-element.41.de) | copy-start | bytes 28311556
  187.8 1.0 copy-start.1
  188.7 1.0 copy-start.2
  189.7 1.0 copy-start.3
  190.7 1.0 copy-start.4
  191.7 0.9 copy-start.5
  192.6 0.7 copy-start.7

commit v3 on v2

--- a/solution.py
+++ b/solution.py
@@ -19,8 +19,8 @@
 TILE = 256
 eps = 1e-6
 FAR = -1e30
-VMEM = 63 << 20
-UNROLL = 2
+VMEM = 253 << 18
+UNROLL = 5
 OUTS = 2
 
 
@@ -247,10 +247,10 @@
         self.o, self.i = self.d // 2, self.d % 2
         self.order = list(range(1, self.lines)) + [0]
 
-    def fill(self, value):
+    def fill(self, value, at=0):
         groups, rows = self.r.shape[0], self.r.shape[1]
         for g in range(groups):
-            self.r[g] = value[g * rows:(g + 1) * rows].astype(bf16)
+            self.r[g, :, at:at + value.shape[1]] = value[g * rows:(g + 1) * rows].astype(bf16)
 
     def target(self, k):
         return (self.o + k) % self.lines
@@ -285,11 +285,20 @@
 
 
 class Queue:
-    def __init__(self, items):
-        self.items = list(items)
-
-    def take(self, gaps):
-        for _ in range(-(-len(self.items) // gaps)):
+    def __init__(self):
+        self.items, self.gaps = [], 1
+
+    def plan(self, items, gaps):
+        self.items += list(items)
+        self.gaps = gaps
+
+    def turn(self):
+        for _ in range(-(-len(self.items) // max(self.gaps, 1))):
+            self.items.pop(0)()
+        self.gaps -= 1
+
+    def rest(self):
+        while self.items:
             self.items.pop(0)()
 
 
@@ -308,7 +317,7 @@
     rows = r.sv.shape[0]
     tiles = r.enc.shape[0] // micros
     span = tiles * TILE
-    steps = tiles + wins - 1
+    steps = -(-(tiles + wins - 1) // UNROLL) * UNROLL
     total = 4 * groups
     lines = groups // 2
     d, m = lax.axis_index("dp"), lax.axis_index("mp")
@@ -354,45 +363,43 @@
     r.a3[m, d, :, 0:192] = r.wv[...]
     r.a3[m, d, :, 192:384] = turned(r.co[...])
     r.b2[d] = r.fo[...]
-    direction = r.dir1[...].astype(f32)
+    direction = unfold_row(r.dir1[...].astype(f32))
     own_dir = jnp.sum(jnp.where(iota((rows, D), 1) == d * rows + iota((rows, D), 0), direction, 0.0), axis=1, keepdims=True)
     r.fd[d] = fold_row(jnp.sum(own_dir * r.fo[...].astype(f32), axis=0, keepdims=True))
 
+    starts = []
     for u in range(micros):
-        def running(p, at, u=u):
+        at, w0 = jnp.int32(0), jnp.int32(0)
+        for p in range(pairs):
             at = at + r.lens[u, 0, p]
-            r.ends[u, p] = at
-            return at
-        lax.fori_loop(0, pairs, running, jnp.int32(0))
-        w0 = jnp.int32(0)
-        for w in range(wins):
-            w0 = w0 + jnp.where(r.ends[u, WIN * w + WIN - 1] <= base, 1, 0)
-
-        def stair(k, carry, u=u):
-            t, w, live, pt, pw = carry
+            if p % WIN == WIN - 1:
+                r.ends[u, p // WIN] = at
+                w0 = w0 + jnp.where(at <= base, 1, 0)
+        starts.append(jnp.minimum(w0, wins - 1))
+
+    def stair(k, carry):
+        out = []
+        for u, (t, w, live, pt, pw, seen) in enumerate(carry):
             r.tk[u, k] = t
             r.wk_[u, k] = w
             r.at[u, k] = jnp.where(live == 1, base + t * TILE, -(1 << 20))
             r.keepw[u, k] = jnp.where(w == pw, 1.0, 0.0)
             r.keept[u, k] = jnp.where(t == pt, 1.0, 0.0)
-            wend, tend = r.ends[u, WIN * w + WIN - 1], base + (t + 1) * TILE
+            seen = [c + jnp.where(x <= i, 1, 0) for c, (x, i) in zip(seen, [(w, i) for i in range(wins)] + [(t, i) for i in range(tiles)])]
+            wend, tend = r.ends[u, w], base + (t + 1) * TILE
             nt = t + jnp.where(wend >= tend, 1, 0)
             nw = w + jnp.where(wend <= tend, 1, 0)
             on = live * jnp.where(nt < tiles, 1, 0)
-            return jnp.where(on == 1, nt, t), jnp.minimum(jnp.where(on == 1, nw, w), wins - 1), on, t, w
-
-        lax.fori_loop(0, steps, stair, (jnp.int32(0), jnp.minimum(w0, wins - 1), jnp.int32(1), jnp.int32(-1), jnp.int32(-1)))
-
-        def last(table, out, count, u=u):
-            def one(i, _):
-                def scan(k, best):
-                    return jnp.where(table[u, k] == i, k, best)
-                out[u, i] = lax.fori_loop(0, steps, scan, jnp.int32(-1))
-                return 0
-            lax.fori_loop(0, count, one, 0)
-
-        last(r.wk_, r.lw, wins)
-        last(r.tk, r.lt, tiles)
+            out.append((jnp.where(on == 1, nt, t), jnp.minimum(jnp.where(on == 1, nw, w), wins - 1), on, t, w, seen))
+        return out
+
+    one, none = jnp.int32(1), jnp.int32(-1)
+    ways = lax.fori_loop(0, steps, stair, [(jnp.int32(0), starts[u], one, none, none, [none] * (wins + tiles)) for u in range(micros)])
+    for u in range(micros):
+        for i in range(wins):
+            r.lw[u, i] = ways[u][5][i]
+        for i in range(tiles):
+            r.lt[u, i] = ways[u][5][wins + i]
     lens = jnp.concatenate([r.lensv[u].astype(f32) for u in range(micros)] + [jnp.zeros((8 - micros, pairs), f32)], axis=0)
     for w in range(wins):
         lane = iota((pairs, 128), 1)
@@ -416,14 +423,16 @@
 
     urgent = A1.events(2.0, 1.5) + A2.events(3.5, 1.5)
     last_one = max(t for t, _ in urgent)
-    later = [(6.0, B1.own), (7.0, F.own), (9.0, A3.own)] + B1.events(9.0, 3.0) + F.events(11.0, 3.0) + A3.events(12.0, 2.0)
+    later = [(5.0, A3.own), (8.0, F.own), (9.0, B1.own)] + A3.events(9.0, 2.0)
+    later += [(14.0 + 2.0 * k, functools.partial(part.arrive, k)) for part in (F, B1) for k in range(1, lines)]
     events = sorted(urgent + later, key=lambda e: e[0])
     for t, e in events:
         if t <= last_one:
             e()
     A1.close()
     A2.close()
-    queue = Queue(e for t, e in events if t > last_one)
+    queue = Queue()
+    queue.plan([e for t, e in events if t > last_one], 6)
 
     def weight_of(ref, k, c0):
         return ref[k, :, :, c0:c0 + WIDE].reshape(D, WIDE)
@@ -451,10 +460,15 @@
 
         return one, two, three
 
-    chunks = ((0, 7), (7, 13), (13, steps))
-
-    def attention(chain, acc):
-        r.chain, r.acc = chain, acc
+    middle = steps // (2 * UNROLL) * UNROLL
+
+    def sweep(*bodies):
+        for a, b in ((0, middle), (middle, steps)):
+            loop(a, b, lambda k: [body(k) for body in bodies])
+            queue.turn()
+
+    def attention(chain):
+        r.chain = chain
         x0 = r.x0[...].reshape(n, D).astype(f32)
         y1b = rms(x0)[0].astype(bf16)
         x1 = x0
@@ -479,103 +493,109 @@
         r.qu[:, :, COLS:128, :] = gap
         r.qu[:, :, 128 + COLS:256, :] = gap
 
-        gaps = 2 * micros * len(chunks)
-
         def tile_rows(u, k):
             return r.enc[u * tiles + r.tk[u, k]]
 
         line = iota((TILE, 128), 0).astype(f32)
-        for u in range(micros):
-            def scores(k, u=u):
-                w = r.wk_[u, k]
-                s = dot(tile_rows(u, k), r.qu[u, w, 0:128, :], 1, 1)
-                at = line + r.at[u, k].astype(f32)
-                s = jnp.where((at >= r.lo[u, w]) & (at < r.hi[u, w]), s, FAR)
-                high = s.astype(bf16)
-                r.da[u, k, :, 0:128] = high
-                r.da[u, k, :, 128:256] = (s - high.astype(f32)).astype(bf16)
-                r.sm[k] = jnp.max(s, axis=0, keepdims=True)
-
-            for a, b in chunks:
-                loop(a, b, scores)
-                queue.take(gaps)
-                gaps -= 1
+
+        def scores(u, k):
+            w = r.wk_[u, k]
+            s = dot(tile_rows(u, k), r.qu[u, w, 0:128, :], 1, 1)
+            at = line + r.at[u, k].astype(f32)
+            s = jnp.where((at >= r.lo[u, w]) & (at < r.hi[u, w]), s, FAR)
+            high = s.astype(bf16)
+            r.ds[u, k] = high
+            r.pa[u, k] = (s - high.astype(f32)).astype(bf16)
+            r.sm[u, k] = jnp.max(s, axis=0, keepdims=True)
+
+        def weights(u, k):
+            w = r.wk_[u, k]
+            s = r.ds[u, k].astype(f32) + r.pa[u, k].astype(f32)
+            p = jnp.where(s > 0.5 * FAR, jnp.exp(s - r.mw[u, w]), 0.0)
+            r.sm[u, k] = jnp.sum(p, axis=0, keepdims=True)
+            low = p.astype(bf16)
+            r.pa[u, k] = low
+            r.chain[k + 1] = dot(low, tile_rows(u, k), 0, 0)[0:COLS] + r.chain[k] * r.keepw[u, k]
+
+        def per_window(u, out, start, join):
             for w in range(wins):
-                top = jnp.full((1, 128), FAR, f32)
+                value = jnp.full((1, 128), start, f32)
                 for k in range(steps):
-                    top = jnp.where(jnp.full((1, 128), r.wk_[u, k]) == w, jnp.maximum(top, r.sm[k]), top)
-                r.mw[u, w] = top
-
-            def weights(k, u=u):
-                w = r.wk_[u, k]
-                s = r.da[u, k, :, 0:128].astype(f32) + r.da[u, k, :, 128:256].astype(f32)
-                p = jnp.where(s > 0.5 * FAR, jnp.exp(s - r.mw[u, w]), 0.0)
-                r.sm[k] = jnp.sum(p, axis=0, keepdims=True)
-                low = p.astype(bf16)
-                r.da[u, k, :, 128:256] = low
-                acc = dot(low, tile_rows(u, k), 0, 0)[0:COLS] + r.acc[0:COLS] * r.keepw[u, k]
-                r.acc[0:COLS] = acc
-                r.chain[k] = acc
-
-            r.acc[...] = jnp.zeros_like(r.acc)
-            for a, b in chunks:
-                loop(a, b, weights)
-                queue.take(gaps)
-                gaps -= 1
-            for w in range(wins):
-                tot = jnp.zeros((1, 128), f32)
-                for k in range(steps):
-                    tot = jnp.where(jnp.full((1, 128), r.wk_[u, k]) == w, tot + r.sm[k], tot)
-                r.lw_[u, w] = tot
-            inv = to_pairs(r.lw_[u].reshape(wins, 128))
-            inv = jnp.where(inv > 0.0, 1.0 / jnp.where(inv > 0.0, inv, 1.0), 0.0)
+                    value = jnp.where(jnp.full((1, 128), r.wk_[u, k]) == w, join(value, r.sm[u, k]), value)
+                out[u, w] = value
+
+        def last_of(u, keep, scale):
             for h in range(HEADS):
                 parts = []
                 for w in range(wins):
-                    k = r.lw[u, w]
-                    part = r.chain[jnp.maximum(k, 0), h * WIN:(h + 1) * WIN, :]
-                    scale = inv[w * WIN:(w + 1) * WIN, h:h + 1]
-                    parts.append(jnp.where(scale > 0.0, part * scale, 0.0))
+                    part = r.chain[r.lw[u, w] + 1, h * WIN:(h + 1) * WIN, :]
+                    here = keep[w * WIN:(w + 1) * WIN, h:h + 1]
+                    if scale is not None:
+                        part = part * scale[w * WIN:(w + 1) * WIN, h:h + 1]
+                    parts.append(jnp.where(here > 0.0, part, 0.0))
                 r.c[h, u * pairs:(u + 1) * pairs, :] = jnp.concatenate(parts, axis=0).astype(bf16)
-        while queue.items:
-            queue.take(1)
+
+        def of(fn, u):
+            return functools.partial(fn, u)
+
+        def contexts(u):
+            per_window(u, r.lw_, 0.0, jnp.add)
+            tot = to_pairs(r.lw_[u].reshape(wins, 128))
+            last_of(u, tot, jnp.where(tot > 0.0, 1.0 / jnp.where(tot > 0.0, tot, 1.0), 0.0))
+
+        sweep(of(scores, 0))
+        for u in range(micros):
+            per_window(u, r.mw, FAR, jnp.maximum)
+            r.chain[0] = jnp.zeros((COLS, D), f32)
+            sweep(of(weights, u), *([of(scores, u + 1)] if u + 1 < micros else []))
+            if u + 1 == micros:
+                B2.own()
+            contexts(u)
+        queue.rest()
         A3.close()
-        B2.own()
         mx = to_pairs(r.mw[...].reshape(micros * wins, 128))
         lx = to_pairs(r.lw_[...].reshape(micros * wins, 128))
-        some = lx > 0.0
-        lse_own = jnp.where(some, mx + jnp.log(jnp.where(some, lx, 1.0)), FAR)
+        some = lx
+        lse_own = jnp.where(lx > 0.0, mx + jnp.log(jnp.where(lx > 0.0, lx, 1.0)), FAR)
         r.mx[...] = mx
         r.lown[...] = lse_own
+        r.lmid[0] = lse_own.T[0:16]
         own = []
         for k in range(4):
             ctx = collapse(dot(r.c[PER * k:PER * (k + 1)].reshape(PER * n, D), weight_of(r.a3, k, 0)), n)
             own.append(ctx)
         fill(r.csend, own)
-        hop = [put(r.csend, r.cbuf0, r.csem.at[0], r.crec.at[0], (d, cm)), put(r.lown, r.lbuf.at[0], r.csem.at[1], r.crec.at[1], (d, cm))]
+        def wide(ref):
+            return jnp.concatenate([ref[...], jnp.zeros((128 - 16, n), f32)], axis=0).T
+
+        hop = [put(r.csend, r.cbuf0, r.csem.at[0], r.crec.at[0], (d, cm)), put(r.lmid.at[0], r.lbuf0, r.csem.at[1], r.crec.at[1], (d, cm))]
         for c in hop:
             c.start()
+        for k in range(lines):
+            F.across(k)
         fd = r.fd[0]
         for g in range(1, groups):
             fd = fd + r.fd[g]
         fd = unfold_row(fd)
         for c in hop:
             c.wait()
-        both, lse = merge(own, lse_own, blocks(r.cbuf0), r.lbuf[0])
+        both, lse = merge(own, lse_own, blocks(r.cbuf0), wide(r.lbuf0))
         fill(r.cmid, both)
-        r.lmid[...] = lse
-        hop = [put(r.cmid, r.cbuf1, r.csem.at[2], r.crec.at[2], (d, xm)), put(r.lmid, r.lbuf.at[1], r.csem.at[3], r.crec.at[3], (d, xm))]
+        r.lmid[1] = lse.T[0:16]
+        hop = [put(r.cmid, r.cbuf1, r.csem.at[2], r.crec.at[2], (d, xm)), put(r.lmid.at[1], r.lbuf1, r.csem.at[3], r.crec.at[3], (d, xm))]
         for c in hop:
             c.start()
         for c in hop:
             c.wait()
-        both, lse = merge(both, lse, blocks(r.cbuf1), r.lbuf[1])
+        both, lse = merge(both, lse, blocks(r.cbuf1), wide(r.lbuf1))
         r.lse[...] = lse
         x2 = r.x1[...]
         for k in range(4):
             low = both[k].astype(bf16)
             r.ctx[k] = low
             x2 = x2 + dot(low, weight_of(r.a3, k, 192), 1, 1)
+        for k in range(lines):
+            B1.across(k)
         ffi = r.b1[...].reshape(D, D)
         y3, r3 = rms(x2)
         y3b = y3.astype(bf16)
@@ -594,6 +614,8 @@
 
         lax.fori_loop(1, total, tell, 0)
         r.hid[...] = hid
+        for k in range(1, lines):
+            B2.arrive(k)
         r.x3[...] = x2.reshape(micros, pairs, D)
 
         heard = r.msgs.at[pl.ds(1, total - 1)]
@@ -643,7 +665,8 @@
         nhop = put(r.nmid.at[1], r.nbuf.at[1], r.nsem.at[1], r.nrec.at[1], (d, xm))
         nhop.start()
         lax.fori_loop(1, groups, scatter, 0)
-        gff = dot(y3b, du, 0, 0)
+        G0.fill(dot(y3b, du, 0, 0))
+        G0.start()
         nhop.wait()
         dn3 = part + r.nbuf[1].astype(f32)
         dx2 = dscore * direction + norm_back(y3, r3, dn3)
@@ -656,8 +679,7 @@
             pick = (iota((WIDE, 128), 0) // HEAD + PER * k == iota((WIDE, 128), 1)).astype(f32)
             delta = delta + exact(dctx.astype(f32) * both[k], pick)
         ones = jnp.ones((n, 64), bf16)
-        G0.fill(jnp.concatenate([gff, dot(gc, r.ctx[m], 0, 0), dot((dn3 * y3).astype(bf16), ones, 0, 0)], axis=1))
-        G0.start()
+        GV.fill(jnp.concatenate([dot(gc, r.ctx[m], 0, 0), dot((dn3 * y3).astype(bf16), ones, 0, 0)], axis=1))
         r.alpha[...] = to_windows(jnp.exp(jnp.minimum(r.mx[...] - lse, 1.0))).reshape(r.alpha.shape)
         r.delta[...] = to_windows(delta).reshape(r.delta.shape)
         share = jnp.exp(jnp.minimum(r.lown[...] - lse, 1.0))
@@ -672,42 +694,32 @@
         v_one()
 
         def value_out():
-            GV.fill(jnp.concatenate([v_three(), jnp.zeros((D, 64), f32)], axis=1))
+            GV.fill(jnp.concatenate([v_three(), jnp.zeros((D, 64), f32)], axis=1), 256)
             GV.start()
 
-        queue.items = [v_two] + G0.events() + [value_out] + [e for _, e in sorted(B2.events(0.0, 1.0), key=lambda e: e[0])] + GV.events()
-        gaps = micros * len(chunks) + 3
-
-        def back(k, u):
+        queue.plan([v_two] + G0.events() + [value_out] + GV.events(), 8)
+
+        def slopes(u, k):
             w = r.wk_[u, k]
-            tile = tile_rows(u, k)
-            da = dot(tile, r.qu[u, w, 128:256, :], 1, 1)
-            a = r.da[u, k, :, 128:256].astype(f32) * r.alpha[u, w]
-            ds = (a * (da - r.delta[u, w])).astype(bf16)
-            r.da[u, k, :, 0:128] = ds
-            r.da[u, k, :, 128:256] = a.astype(bf16)
-            acc = dot(ds, tile, 0, 0)[0:COLS] + r.acc[0:COLS] * r.keepw[u, k]
-            r.acc[0:COLS] = acc
-            r.chain[k] = acc
-
+            da = dot(tile_rows(u, k), r.qu[u, w, 128:256, :], 1, 1)
+            a = r.pa[u, k].astype(f32) * r.alpha[u, w]
+            r.ds[u, k] = (a * (da - r.delta[u, w])).astype(bf16)
+
+        def sums_of(u, k):
+            r.chain[k + 1] = dot(r.ds[u, k], tile_rows(u, k), 0, 0)[0:COLS] + r.chain[k] * r.keepw[u, k]
+
+        sweep(of(slopes, 0))
         for u in range(micros):
-            r.acc[...] = jnp.zeros_like(r.acc)
-            for a, b in chunks:
-                loop(a, b, lambda k, u=u: back(k, u))
-                queue.take(gaps)
-                gaps -= 1
-            for h in range(HEADS):
-                parts = []
-                for w in range(wins):
-                    k = r.lw[u, w]
-                    parts.append(jnp.where(jnp.full((WIN, D), k) >= 0, r.chain[jnp.maximum(k, 0), h * WIN:(h + 1) * WIN, :], 0.0))
-                r.c[h, u * pairs:(u + 1) * pairs, :] = jnp.concatenate(parts, axis=0).astype(bf16)
-
-    pl.run_scoped(attention, pltpu.VMEM((steps, COLS, D), f32), pltpu.VMEM((128, D), f32))
-
-    def rest_of_it(r1, ys1, full, out):
-        r.r1, r.ys1, r.full, r.out = r1, ys1, full, out
+            r.chain[0] = jnp.zeros((COLS, D), f32)
+            sweep(of(sums_of, u), *([of(slopes, u + 1)] if u + 1 < micros else []))
+            last_of(u, some[u * pairs:(u + 1) * pairs], None)
+
+    pl.run_scoped(attention, pltpu.VMEM((steps + 1, COLS, D), f32))
+
+    def rest_of_it(r1, ys1, r3, ys3, full, out):
+        r.r1, r.ys1, r.r3, r.ys3, r.full, r.out = r1, ys1, r3, ys3, full, out
         G1 = Reduce(r.r1, r.yr1, r.ys1, r.z1, (r.snd1, r.yrec1, r.zrec1))
+        GK = Reduce(r.r3, r.yr3, r.ys3, r.z3, (r.snd3, r.yrec3, r.zrec3))
         part = [collapse(dot(r.c[PER * k:PER * (k + 1)].reshape(PER * n, D), weight_of(r.a2, k, 192)), n) for k in range(4)]
         fill(r.csend, part)
         hop = put(r.csend, r.cbuf0, r.qsem.at[0], r.qrec.at[0], (d, cm))
@@ -721,8 +733,9 @@
         hop = put(r.cmid, r.cbuf1, r.qsem.at[1], r.qrec.at[1], (d, xm))
         hop.start()
         k_one()
-        while queue.items:
-            queue.take(1)
+        queue.rest()
+        for k in range(lines):
+            B2.across(k)
         x3p = dot(r.hid[...], r.b2[...].reshape(D, D), 1, 1)
         r.nmid[0] = x3p.astype(bf16)
         xhop = put(r.nmid.at[0], r.nbuf.at[0], r.xsem.at[0], r.xrec.at[0], (d, cm))
@@ -749,15 +762,16 @@
         half_ones = jnp.where(iota((n, 64), 1) < 32, ones, 0)
         small = [dot(y1.astype(bf16), r.dctx[m], 0, 0), dot(gs, r.v1[m], 0, 0), dot(y2.astype(bf16), r.dq[m], 0, 0)]
         tail = dot((dn1 * y1).astype(bf16), half_ones, 0, 0) + dot((dn2 * y2).astype(bf16), ones - half_ones, 0, 0)
-        G1.fill(jnp.concatenate(small + [k_three(), tail, jnp.zeros((D, 64), f32)], axis=1))
+        G1.fill(jnp.concatenate(small + [tail], axis=1))
         G1.start()
+        GK.fill(jnp.concatenate([k_three(), jnp.zeros((D, 64), f32)], axis=1))
+        GK.start()
         xhop.wait()
         x3p = x3p + r.nbuf[0].astype(f32)
         r.nmid[1] = x3p.astype(bf16)
         xhop = put(r.nmid.at[1], r.nbuf.at[1], r.xsem.at[1], r.xrec.at[1], (d, xm))
         xhop.start()
-        queue.items += G1.events()
-        gaps = micros * 4
+        queue.plan(G1.events() + GK.events(), micros * 2)
 
         def rows_out(u, t, slot):
             return pltpu.make_async_copy(r.out.at[slot], r.de.at[u, pl.ds(t * TILE, TILE), :], r.osem.at[slot])
@@ -765,10 +779,8 @@
         for u in range(micros):
             if u == 0:
                 r.full[...] = jnp.zeros_like(r.full)
-            for a, b in ((0, 10), (10, steps)):
-                loop(a, b, functools.partial(place, r, u))
-                queue.take(gaps)
-                gaps -= 1
+            loop(0, steps, functools.partial(place, r, u))
+            queue.turn()
             for t in range(tiles):
                 slot = (u * tiles + t) % OUTS
                 if u * tiles + t >= OUTS:
@@ -777,12 +789,10 @@
                 r.out[slot] = r.enc[k]
                 rows_out(u, t, slot).start()
                 if t % 6 == 5:
-                    queue.take(gaps)
-                    gaps -= 1
+                    queue.turn()
         for slot in range(OUTS):
             rows_out(micros - 1, tiles - 1, slot).wait()
-        while queue.items:
-            queue.take(1)
+        queue.rest()
 
         heard = r.hsum.at[pl.ds(1, groups - 1)]
         put(heard, heard, r.hsem.at[0], r.hsem.at[1], (d, cm)).wait()
@@ -795,14 +805,18 @@
         r.out0[...] = G0.finish()
         r.out2[...] = GV.finish()
         r.out1[...] = G1.finish()
-
-    pl.run_scoped(rest_of_it, pltpu.VMEM((groups, rows, 896), bf16), pltpu.VMEM((lines, rows, 896), bf16), pltpu.VMEM((TILE, D), f32), pltpu.VMEM((OUTS, TILE, D), bf16))
+        r.out3[...] = GK.finish()
+
+    pl.run_scoped(rest_of_it, pltpu.VMEM((groups, rows, 640), bf16), pltpu.VMEM((lines, rows, 640), bf16),
+                  pltpu.VMEM((groups, rows, 256), bf16), pltpu.VMEM((lines, rows, 256), bf16), pltpu.VMEM((TILE, D), f32), pltpu.VMEM((OUTS, TILE, D), bf16))
     for part in (A1, A2, A3, B1, B2, F):
         part.sent()
 
 
 def place(r, u, k):
-    acc = dot(r.da[u, k], r.qu[u, r.wk_[u, k]]) + r.full[...] * r.keept[u, k]
+    w = r.wk_[u, k]
+    a = (r.pa[u, k].astype(f32) * r.alpha[u, w]).astype(bf16)
+    acc = dot(jnp.concatenate([r.ds[u, k], a], axis=1), r.qu[u, w]) + r.full[...] * r.keept[u, k]
     r.full[...] = acc
     r.enc[k] = acc.astype(bf16)
 
@@ -812,7 +826,7 @@
     n, wins, rows, lines = micros * pairs, pairs // WIN, sv.shape[0], groups // 2
     span = encoded.shape[1] // 4
     tiles = span // TILE
-    steps = tiles + wins - 1
+    steps = -(-(tiles + wins - 1) // UNROLL) * UNROLL
     sd = jax.ShapeDtypeStruct
     any_, vm, sm = (pl.BlockSpec(memory_space=s) for s in (pl.ANY, pltpu.VMEM, pltpu.SMEM))
     S, V, M = pltpu.SemaphoreType.DMA, pltpu.VMEM, pltpu.SMEM
@@ -820,18 +834,18 @@
                sv=sv, so=so, wq=wq, wk=wk, wv=wv, co=co, fi=fi, fo=fo)
     places = dict(enc_hbm=any_, lens=sm)
     outs = dict(x3=sd((micros, pairs, D), f32), dx0=sd((micros, pairs, D), f32), de=sd((micros, span, D), bf16), hs=sd((8, 128), f32),
-                out0=sd((rows, 1024), f32), out1=sd((rows, 896), f32), out2=sd((rows, 256), f32))
+                out0=sd((rows, D), f32), out1=sd((rows, 640), f32), out2=sd((rows, 512), f32), out3=sd((rows, 256), f32))
     places.update(de=any_)
     scratch = dict(
         enc=V((max(micros * tiles, steps), TILE, D), bf16), esem=S((micros,)),
         a1=V((4, groups, rows, 384), bf16), a2=V((4, groups, rows, 384), bf16), a3=V((4, groups, rows, 384), bf16),
         b1=V((groups, rows, D), bf16), b2=V((groups, rows, D), bf16), fd=V((groups, 8, 128), f32), hid=V((n, D), bf16),
-        ends=M((micros, pairs), jnp.int32), tk=M((micros, steps), jnp.int32), wk_=M((micros, steps), jnp.int32), at=M((micros, steps), jnp.int32),
+        ends=M((micros, wins), jnp.int32), tk=M((micros, steps), jnp.int32), wk_=M((micros, steps), jnp.int32), at=M((micros, steps), jnp.int32),
         keepw=M((micros, steps), f32), keept=M((micros, steps), f32), lw=M((micros, wins), jnp.int32), lt=M((micros, tiles), jnp.int32),
         lo=V((micros, wins, 1, 128), f32), hi=V((micros, wins, 1, 128), f32), slotr=V((groups, n), jnp.int32),
-        x1=V((n, D), f32), v1=V((4, n, WIDE), bf16), q=V((4, n, WIDE), bf16), qu=V((micros, wins, 256, D), bf16), sm=V((steps, 1, 128), f32), mw=V((micros, wins, 1, 128), f32), lw_=V((micros, wins, 1, 128), f32),
-        da=V((micros, steps, TILE, 256), bf16), c=V((HEADS, n, D), bf16), mx=V((n, 128), f32), lown=V((n, 128), f32), lse=V((n, 128), f32),
-        csend=V((2, n, 384), bf16), cmid=V((2, n, 384), bf16), cbuf0=V((2, n, 384), bf16), cbuf1=V((2, n, 384), bf16), lmid=V((n, 128), f32), lbuf=V((2, n, 128), f32),
+        x1=V((n, D), f32), v1=V((4, n, WIDE), bf16), q=V((4, n, WIDE), bf16), qu=V((micros, wins, 256, D), bf16), sm=V((micros, steps, 1, 128), f32), mw=V((micros, wins, 1, 128), f32), lw_=V((micros, wins, 1, 128), f32),
+        ds=V((micros, steps, TILE, 128), bf16), pa=V((micros, steps, TILE, 128), bf16), c=V((HEADS, n, D), bf16), mx=V((n, 128), f32), lown=V((n, 128), f32), lse=V((n, 128), f32),
+        csend=V((2, n, 384), bf16), cmid=V((2, n, 384), bf16), cbuf0=V((2, n, 384), bf16), cbuf1=V((2, n, 384), bf16), lmid=V((2, 16, n), f32), lbuf0=V((16, n), f32), lbuf1=V((16, n), f32),
         csem=S((4,)), crec=S((4,)), ctx=V((4, n, WIDE), bf16), msgs=V((4 * groups, 8, n), f32), msem=S((2,)),
         xsem=S((2,)), xrec=S((2,)), nmid=V((2, n, D), bf16), nbuf=V((2, n, D), bf16), nsem=S((2,)), nrec=S((2,)),
         hsum=V((groups, 8, 128), f32), hsem=S((2,)), dx2=V((n, D), f32), dctx=V((4, n, WIDE), bf16), dq=V((4, n, WIDE), bf16),
@@ -844,9 +858,9 @@
         scratch.update({"s" + part: S((5,)), "z" + part: S((lines,)), "y" + part: S((lines,))})
         if part[0] == "a":
             scratch.update({"x" + part: S((groups,)), "c" + part: S((2,)), "q" + part: S((lines,))})
-    for tag, columns in (("0", 1024), ("1", 896), ("2", 256)):
+    for tag, columns in (("0", 768), ("1", 640), ("2", 512), ("3", 256)):
         piece = lambda k: V((k, rows, columns), bf16)
-        if tag != "1":
+        if tag in "02":
             scratch.update({"r" + tag: piece(groups), "ys" + tag: piece(lines)})
         scratch.update({"yr" + tag: piece(lines), "z" + tag: piece(lines - 1),
                         "snd" + tag: S((2,)), "yrec" + tag: S((lines,)), "zrec" + tag: S((lines - 1,))})
@@ -861,63 +875,80 @@
     )(*ins.values())
 
 
-def outputs_kernel(dir_ref, hs, out0, out1, out2, g1, g2, g3, x3, dx0, de,
-                   g_self, g_cross, g_ff, self_value, self_out, query, key, value, cross_out, ff_in, ff_out, x3_out, dx0_out, de_out, room, sem):
-    parts = de.shape[1] // 768
-    every = [(u, pl.ds(k * 768, 768), u * parts + k) for u in range(de.shape[0]) for k in range(parts)]
+def outputs_kernel(count, dir_ref, g1, g2, g3, *refs):
+    sums, de = refs[:7], refs[7]
+    outs, de_out = refs[8:21], refs[21]
+    hs, out0, out1, out2, out3 = refs[22:27]
+    made, (room, sem, hsem, osem) = refs[27:40], refs[40:]
+    (g_self, g_cross, g_ff, self_value, self_out, query, key, value, cross_out, ff_in, ff_out, x3_out, dx0_out) = made
+    leave = [pltpu.make_async_copy(src, dst, osem.at[k]) for k, (src, dst) in enumerate(zip(made, outs))]
+    near = [pltpu.make_async_copy(src, dst, hsem.at[k]) for k, (src, dst) in enumerate(zip(sums, (hs, out0, out1, out2, out3, x3_out, dx0_out)))]
+    for c in near:
+        c.start()
+    height = room.shape[1]
+    parts = de.shape[1] // height
+    every = [(u, pl.ds(k * height, height), u * parts + k) for u in range(de.shape[0]) for k in range(parts)]
     loads = [pltpu.make_async_copy(de.at[u, at], room.at[k], sem.at[0, k]) for u, at, k in every]
     stores = [pltpu.make_async_copy(room.at[k], de_out.at[u, at], sem.at[1, k]) for u, at, k in every]
     for c in loads:
         c.start()
     rows = out0.shape[0]
     columns = [to_column(g[...].astype(f32)) for g in (g1, g2, g3)]
-    g_self[...] = to_row(out1[:, 768:769] / columns[0])
-    g_cross[...] = to_row(out1[:, 800:801] / columns[1])
-    g_ff[...] = to_row(out0[:, 960:961] / columns[2])
+    mine = iota((rows, D), 1) == lax.axis_index("dp") * rows + iota((rows, D), 0)
+    own_dir = jnp.sum(jnp.where(mine, unfold_row(dir_ref[...].astype(f32)), 0.0), axis=1, keepdims=True)
+    for c in near:
+        c.wait()
+    for c, back in list(zip(loads, stores))[:count // 2]:
+        c.wait()
+        back.start()
+    g_self[...] = to_row(out1[:, 576:577] / columns[0])
+    g_cross[...] = to_row(out1[:, 608:609] / columns[1])
+    g_ff[...] = to_row(out2[:, 192:193] / columns[2])
     self_value[...] = out1[:, 0:192] * columns[0]
     self_out[...] = out1[:, 192:384].T
     query[...] = out1[:, 384:576] * columns[1]
-    key[...] = out1[:, 576:768]
-    value[...] = out2[:, 0:192]
-    cross_out[...] = out0[:, 768:960].T
-    ff_in[...] = out0[:, 0:768] * columns[2]
-    mine = iota((rows, D), 1) == lax.axis_index("dp") * rows + iota((rows, D), 0)
-    own_dir = jnp.sum(jnp.where(mine, dir_ref[...].astype(f32), 0.0), axis=1, keepdims=True)
+    key[...] = out3[:, 0:192]
+    value[...] = out2[:, 256:448]
+    cross_out[...] = out2[:, 0:192].T
+    ff_in[...] = out0[...] * columns[2]
     ff_out[...] = own_dir * unfold_row(hs[...])
-    x3_out[...] = x3[...]
-    dx0_out[...] = dx0[...]
-    for c, back in zip(loads, stores):
+    for c in leave:
+        c.start()
+    for c, back in list(zip(loads, stores))[count // 2:]:
         c.wait()
         back.start()
-    for c in stores:
+    for c in stores + leave:
         c.wait()
 
 
-def outputs(dir1, hs, out0, out1, out2, g1, g2, g3, x3, dx0, de):
-    rows, count = out0.shape[0], de.shape[0] * de.shape[1] // 768
+def outputs(dir1, gains, hs, out0, out1, out2, out3, x3, dx0, de):
+    rows, height = out0.shape[0], 512
+    count = de.shape[0] * de.shape[1] // height
     sd = jax.ShapeDtypeStruct
     tall, flat = sd((rows, WIDE), f32), sd((WIDE, rows), f32)
     any_, vm = (pl.BlockSpec(memory_space=s) for s in (pl.ANY, pltpu.VMEM))
+    shapes = (sd((1, rows), f32),) * 3 + (tall, flat, tall, tall, tall, flat, sd((rows, D), f32), sd((rows, D), f32), sd(x3.shape, f32), sd(x3.shape, f32))
     return pl.pallas_call(
-        outputs_kernel,
-        out_shape=(sd((1, rows), f32),) * 3 + (tall, flat, tall, tall, tall, flat, sd((rows, D), f32), sd((rows, D), f32),
-                                               sd(x3.shape, f32), sd(x3.shape, f32), sd(de.shape, bf16)),
-        in_specs=[vm] * 10 + [any_], out_specs=[vm] * 13 + [any_],
-        scratch_shapes=[pltpu.VMEM((count, 768, D), bf16), pltpu.SemaphoreType.DMA((2, count))],
-        compiler_params=pltpu.CompilerParams(vmem_limit_bytes=32 << 20),
+        functools.partial(outputs_kernel, count),
+        out_shape=shapes + (sd(de.shape, bf16),),
+        in_specs=[vm] * 4 + [any_] * 8, out_specs=[any_] * 14,
+        scratch_shapes=[pltpu.VMEM(x.shape, f32) for x in (hs, out0, out1, out2, out3) + shapes] +
+                       [pltpu.VMEM((count, height, D), bf16), pltpu.SemaphoreType.DMA((2, count)), pltpu.SemaphoreType.DMA((7,)),
+                        pltpu.SemaphoreType.DMA((len(shapes),))],
+        compiler_params=pltpu.CompilerParams(vmem_limit_bytes=VMEM),
         name="outputs",
-    )(dir1, hs, out0, out1, out2, g1, g2, g3, x3, dx0, de)
+    )(dir1, *gains, hs, out0, out1, out2, out3, x3, dx0, de)
 
 
 def shards(dec_in, encoded, seg_lengths, pair_slot, relevance, score_dir, gain_self, gain_cross, gain_ff,
            self_value, self_out, cross_query, cross_key, cross_value, cross_out, ff_in, ff_out):
     groups = lax.axis_size("dp")
     gains = [g.reshape(1, -1) for g in (gain_self, gain_cross, gain_ff)]
-    dir1 = score_dir.reshape(1, D)
-    x3, dx0, d_encoded, hs, out0, out1, out2 = layer(
+    dir1 = score_dir.reshape(D // 128, 128)
+    x3, dx0, d_encoded, hs, out0, out1, out2, out3 = layer(
         groups, CAND * math.sqrt(D), dec_in, encoded, seg_lengths, pair_slot, relevance, dir1, *gains,
         self_value, self_out, cross_query, cross_key, cross_value, cross_out, ff_in, ff_out.T)
-    g1, g2, g3, *weights, x3, dx0, d_encoded = outputs(dir1, hs, out0, out1, out2, *gains, x3, dx0, d_encoded)
+    g1, g2, g3, *weights, x3, dx0, d_encoded = outputs(dir1, gains, hs, out0, out1, out2, out3, x3, dx0, d_encoded)
     weights[-1] = weights[-1].T
     return (x3, dx0, d_encoded, g1.reshape(-1), g2.reshape(-1), g3.reshape(-1), *weights)
 

time: 201 us -> 159 us (0.79)
  Pallas kernels: 190 us -> 158 us
  local copies, waits for them, and re-layouts: 10.5 us -> 0 us
    pallas_call x1, Pallas kernels: 182 us -> 148 us  [layer(): pl.pallas_call(functools.partial(layer_kernel, groups, weight, names), ou...]
    unnamed x22 -> x0, local copies, waits for them, and re-layouts: 9.22 us -> none
where the time goes in v3:
time: 159 us
  Pallas kernels  158 us (99%)
    pallas_call x1, Pallas kernels, layer(): pl.pallas_call(functools.partial(layer_kernel, groups, weight, names), ou...  148 us
    pallas_call x1, Pallas kernels, outputs(): pl.pallas_call(functools.partial(outputs_kernel, count), out_shape=shapes...  9.25 us

profile of v3, /device:TPU:0, one launch (start us, length us, event | category | flops | bytes accessed | tf_op | source)
XLA Modules:
  0.0 158.5 jit_solution(13468212532594829148)
XLA Ops:
  0.7 148.4 %decoder_layer.1 = (f32[2,64,768]{2,1,0:T(8,128)}, f32[2,64,768]{2,1,0:T(8,128)}, bf16[2,3072,768]{2,1,0:T(8,128)(2,1)}, f32[8,128]{1,0:T(8,128)}, f32[96,768]{1...) custom-call(bf16[2,64,768]{2,1,0:T(8,128)(2,1)} %refs_0_.1, bf16[2,12288,768]{2,1,0:T(8,128)(2,1)} %refs_1_.1, ...), custom_call_target="tpu_custom_call" | custom-call | tf_op jit(solution)/shard_map/decoder_layer/pallas_call | solution.py:868
  149.1 9.3 %outputs.1 = (f32[1,96]{1,0:T(1,128)}, f32[1,96]{1,0:T(1,128)}, f32[1,96]{1,0:T(1,128)}, f32[96,192]{1,0:T(8,128)}, f32[192,96]{1,0:T(8,128)}, /*index=5*/f32[96...) custom-call(bf16[6,128]{1,0:T(8,128)(2,1)} %bitcast.11, ...), custom_call_target="tpu_custom_call" | custom-call | tf_op jit(solution)/shard_map/outputs/pallas_call | solution.py:931
